TPU v7x, 128 devices: a whole 4x4x4 slice. The times are simulated.
128 devices in a mesh: dp: 16 (over y_lo, x, core), tensor: 8 (over y_hi, z).
Axes of the slice: x: 4, y: 4 (y_hi: 2, y_lo: 2; y = y_hi * 2 + y_lo), z: 4, core: 2. Of those that a mesh axis runs over, the one named last changes fastest.
Arguments:
- picture_encoder_result: bfloat16 [5632, 1024], P('dp'), may hold values from -0.59765625 to 0.59765625
- sentence_encoder_result: bfloat16 [22528, 1024], P(('dp', 'tensor')), may hold values from -0.59765625 to 0.59765625
- picture_projector_matrix: bfloat16 [1024, 1024], P(None, 'tensor'), may hold values from -0.1875 to 0.1875
- sentence_projector_matrix: bfloat16 [1024, 1024], P(None, 'tensor'), may hold values from -0.1875 to 0.1875
- sentences_for_picture: int32 [5632], replicated, may hold values from 1 to 8, 22528 in all
- sharpness_factor: float32 [1], replicated, may hold values from 30 to 60
- score_offset_term: float32 [1], replicated, may hold values from -8 to -4
Outputs:
- grad_img: bfloat16 [5632, 1024], P('dp', 'tensor')
- grad_cap: bfloat16 [22528, 1024], P(('dp', 'tensor'))
Inputs may be any that keep to these rules, and one draw needn't show every extreme that they name: The counts sum to 22528; the captions of image m are the consecutive rows start[m] to start[m] + sentences_for_picture[m] - 1 of sentence_encoder_result, where start[m] is the sum of the counts of images before m; some image has 8.
All inputs are finite; a program needn't handle non-finite values.
Results may differ from a plain program's by a relative error of at most 0.014.
Values may be sent and summed in bfloat16 or wider, within the bound.
A program may use at most 64 MiB of HBM per device.

v0:
```python
import jax
import jax.numpy as jnp
from jax import lax
from jax.sharding import PartitionSpec as P

epsilon = 1e-06


def passed_along(value, axis, steps):
    count = lax.axis_size(axis)
    pairs = [(source, (source + steps) % count) for source in range(count)]
    return lax.ppermute(value, axis, pairs)


def embed(features, loss_multiplier):
    raw = jnp.dot(features, loss_multiplier, preferred_element_type=jnp.float32)
    scale = lax.rsqrt(jnp.sum(raw * raw, axis=1, keepdims=True) + epsilon)
    return (raw * scale, scale)


def scaling_factor(
    similarity_matrix,
    other_begin_list,
    sentence_tally_later,
    other_position,
    scaled_sharpness,
    displacement,
):
    raw_similarity = scaled_sharpness * similarity_matrix + displacement
    inside = (other_position >= other_begin_list) & (
        other_position < other_begin_list + sentence_tally_later
    )
    match_polarity = jnp.where(inside, 1.0, -1.0)
    loss_multiplier = jnp.where(inside, 1.0 / sentence_tally_later.astype(jnp.float32), 1.0)
    return (
        scaled_sharpness
        * (-match_polarity * loss_multiplier * jax.nn.sigmoid(-match_polarity * raw_similarity))
    ).astype(jnp.bfloat16)


def unit_back(grad, unit, scale):
    return scale * (grad - unit * jnp.sum(unit * grad, axis=1, keepdims=True))


def divided_product(values, loss_multiplier):
    upper = lax.optimization_barrier(values.astype(jnp.bfloat16))
    lower = (values - upper.astype(jnp.float32)).astype(jnp.bfloat16)
    first = jnp.einsum("me,de->md", upper, loss_multiplier, preferred_element_type=jnp.float32)
    return first + jnp.einsum(
        "me,de->md", lower, loss_multiplier, preferred_element_type=jnp.float32
    )


def body(
    picture_encoder_result,
    sentence_encoder_result,
    picture_projector_matrix,
    sentence_projector_matrix,
    sentences_for_picture,
    sharpness_factor,
    score_offset_term,
):
    full_img, full_cap = (
        lax.all_gather(picture_projector_matrix, "tensor", axis=1, tiled=True),
        lax.all_gather(sentence_projector_matrix, "tensor", axis=1, tiled=True),
    )
    img_unit, img_scale = embed(picture_encoder_result, full_img)
    cap_unit, cap_scale = embed(sentence_encoder_result, full_cap)
    img_z = img_unit.astype(jnp.bfloat16)
    cap_z = cap_unit.astype(jnp.bfloat16)
    scaled_sharpness = sharpness_factor[0]
    displacement = score_offset_term[0]
    ends = jnp.cumsum(sentences_for_picture)
    starts = ends - sentences_for_picture
    cycle_count = lax.axis_size("dp")
    tensor_count = lax.axis_size("tensor")
    cycle_pos = lax.axis_index("dp")
    tensor_pos = lax.axis_index("tensor")
    img_rows = picture_encoder_result.shape[0]
    cap_rows = sentence_encoder_result.shape[0]
    width = img_z.shape[1]
    row_iota = jnp.arange(cap_rows, dtype=jnp.int32)
    sentence_number = (cycle_pos * tensor_count + tensor_pos) * cap_rows + row_iota

    def block_of(anchor):
        first = anchor * img_rows
        group_begin_list = lax.dynamic_slice_in_dim(starts, first, img_rows)
        group_sizes_list = lax.dynamic_slice_in_dim(sentences_for_picture, first, img_rows)
        return (group_begin_list, group_sizes_list)

    def image_tile(block_z, anchor):
        group_begin_list, group_sizes_list = block_of(anchor)
        similarity_matrix = jnp.einsum(
            "me,ce->mc", block_z, cap_z, preferred_element_type=jnp.float32
        )
        return scaling_factor(
            similarity_matrix,
            group_begin_list[:, None],
            group_sizes_list[:, None],
            sentence_number[None, :],
            scaled_sharpness,
            displacement,
        )

    def step(turn, state):
        block_z, carried, cap_grad = state
        anchor = (cycle_pos - turn) % cycle_count
        pair_factor = image_tile(block_z, anchor)
        cap_grad = cap_grad + jnp.einsum(
            "mc,me->ce", pair_factor, block_z, preferred_element_type=jnp.float32
        )
        carried = carried + jnp.dot(pair_factor, cap_z, preferred_element_type=jnp.float32)
        carried = passed_along(carried.astype(jnp.bfloat16), "dp", 1).astype(carried.dtype)
        block_z = passed_along(block_z, "dp", 1)
        return (block_z, carried, cap_grad)

    start_state = (
        img_z,
        jnp.zeros((img_rows, width), jnp.float32),
        jnp.zeros((cap_rows, width), jnp.float32),
    )
    unused, img_grad, cap_grad = lax.fori_loop(0, cycle_count, step, start_state)
    img_back = unit_back(img_grad, img_unit, img_scale)
    img_part = divided_product(img_back, full_img)
    grad_img = lax.psum_scatter(
        img_part.astype(jnp.bfloat16), "tensor", scatter_dimension=1, tiled=True
    )
    cap_back = unit_back(cap_grad, cap_unit, cap_scale)
    grad_cap = divided_product(cap_back, full_cap)
    return (grad_img, grad_cap.astype(jnp.bfloat16))


def solution(mesh):
    in_specs = (
        P("dp", None),
        P(("dp", "tensor"), None),
        P(None, "tensor"),
        P(None, "tensor"),
        P(),
        P(),
        P(),
    )
    out_specs = (P("dp", "tensor"), P(("dp", "tensor"), None))
    return jax.shard_map(body, mesh=mesh, in_specs=in_specs, out_specs=out_specs, check_vma=False)
```

profile of v0, /device:TPU:0, one launch (start us, length us, event | category | flops | bytes accessed | tf_op | source)
XLA Modules:
  0.0 632.3 jit_solution(152464883537165580)
XLA Ops:
  10.8 56.4 %all-gather.5.cloned.1.call-done = bf16[1024,1024]{1,0:T(8,128)(2,1)} async-done(((bf16[1024,128]{1,0:T(8,128)(2,1)}), bf16[1024,1024]{1,0:T(8,128)(2,1)}) %all-gather.5.cloned.1.call-update) | async-done | bytes 2097168 | tf_op jit(solution)/shard_map/all_gather | solution.py:65
  67.3 2.4 multiply_reduce_fusion.3
  69.7 52.2 %all-gather.3.cloned.1.call-done = bf16[1024,1024]{1,0:T(8,128)(2,1)} async-done(((bf16[1024,128]{1,0:T(8,128)(2,1)}), bf16[1024,1024]{1,0:T(8,128)(2,1)}) %all-gather.3.cloned.1.call-update) | async-done | bytes 2097168 | tf_op jit(solution)/shard_map/all_gather | solution.py:64
  121.9 2.6 multiply_reduce_fusion.1
  125.9 424.6 %while.20 = (s32[]{:T(128)}, bf16[352,1024]{1,0:T(8,128)(2,1)}, f32[352,1024]{1,0:T(8,128)S(1)}, f32[176,1024]{1,0:T(8,128)}, f32[]{:T(128)}, /*index=5*/s32[]{:...) while((s32[]{:T(128)}, bf16[352,1024]{1,0:T(8,128)(2,1)}, ...), condition=%wide.region_5.6_spmd.clone, body=%wide.region_4.5_spmd.clone.sunk | while | flops 383427808 | bytes 15525043 | solution.py:122
  128.5 1.8 fusion.48
  134.4 10.3 %collective-permute-done.1 = bf16[352,1024]{1,0:T(8,128)(2,1)} collective-permute-done((bf16[352,1024]{1,0:T(8,128)(2,1)}, bf16[352,1024]{1,0:T(8,128)(2,1)}, u32[]{:S(2)}, u32[]{:S(2)}) %collective-permute-start.1) | collective-permute-done | bytes 720928 | tf_op jit(solution)/shard_map/while/body/eval_jaxpr/ppermute | solution.py:12
  146.0 6.5 %collective-permute-done = bf16[352,1024]{1,0:T(8,128)(2,1)} collective-permute-done((bf16[352,1024]{1,0:T(8,128)(2,1)S(1)}, bf16[352,1024]{1,0:T(8,128)(2,1)}, u32[]{:S(2)}, u32[]{:S(2)}) %collective-permute-start) | collective-permute-done | bytes 720928 | tf_op jit(solution)/shard_map/while/body/eval_jaxpr/ppermute | solution.py:12
  155.1 1.8 fusion.48
  158.1 2.3 convolution_add_fusion.5
  160.4 10.8 %collective-permute-done.1 = bf16[352,1024]{1,0:T(8,128)(2,1)} collective-permute-done((bf16[352,1024]{1,0:T(8,128)(2,1)}, bf16[352,1024]{1,0:T(8,128)(2,1)}, u32[]{:S(2)}, u32[]{:S(2)}) %collective-permute-start.1) | collective-permute-done | bytes 720928 | tf_op jit(solution)/shard_map/while/body/eval_jaxpr/ppermute | solution.py:12
  172.5 6.5 %collective-permute-done = bf16[352,1024]{1,0:T(8,128)(2,1)} collective-permute-done((bf16[352,1024]{1,0:T(8,128)(2,1)S(1)}, bf16[352,1024]{1,0:T(8,128)(2,1)}, u32[]{:S(2)}, u32[]{:S(2)}) %collective-permute-start) | collective-permute-done | bytes 720928 | tf_op jit(solution)/shard_map/while/body/eval_jaxpr/ppermute | solution.py:12
  181.6 1.8 fusion.48
  184.6 2.3 convolution_add_fusion.5
  187.0 10.8 %collective-permute-done.1 = bf16[352,1024]{1,0:T(8,128)(2,1)} collective-permute-done((bf16[352,1024]{1,0:T(8,128)(2,1)}, bf16[352,1024]{1,0:T(8,128)(2,1)}, u32[]{:S(2)}, u32[]{:S(2)}) %collective-permute-start.1) | collective-permute-done | bytes 720928 | tf_op jit(solution)/shard_map/while/body/eval_jaxpr/ppermute | solution.py:12
  199.0 6.5 %collective-permute-done = bf16[352,1024]{1,0:T(8,128)(2,1)} collective-permute-done((bf16[352,1024]{1,0:T(8,128)(2,1)S(1)}, bf16[352,1024]{1,0:T(8,128)(2,1)}, u32[]{:S(2)}, u32[]{:S(2)}) %collective-permute-start) | collective-permute-done | bytes 720928 | tf_op jit(solution)/shard_map/while/body/eval_jaxpr/ppermute | solution.py:12
  208.2 1.8 fusion.48
  211.2 2.3 convolution_add_fusion.5
  213.5 10.8 %collective-permute-done.1 = bf16[352,1024]{1,0:T(8,128)(2,1)} collective-permute-done((bf16[352,1024]{1,0:T(8,128)(2,1)}, bf16[352,1024]{1,0:T(8,128)(2,1)}, u32[]{:S(2)}, u32[]{:S(2)}) %collective-permute-start.1) | collective-permute-done | bytes 720928 | tf_op jit(solution)/shard_map/while/body/eval_jaxpr/ppermute | solution.py:12
  225.6 6.5 %collective-permute-done = bf16[352,1024]{1,0:T(8,128)(2,1)} collective-permute-done((bf16[352,1024]{1,0:T(8,128)(2,1)S(1)}, bf16[352,1024]{1,0:T(8,128)(2,1)}, u32[]{:S(2)}, u32[]{:S(2)}) %collective-permute-start) | collective-permute-done | bytes 720928 | tf_op jit(solution)/shard_map/while/body/eval_jaxpr/ppermute | solution.py:12
  237.7 2.3 convolution_add_fusion.5
  240.1 10.8 %collective-permute-done.1 = bf16[352,1024]{1,0:T(8,128)(2,1)} collective-permute-done((bf16[352,1024]{1,0:T(8,128)(2,1)}, bf16[352,1024]{1,0:T(8,128)(2,1)}, u32[]{:S(2)}, u32[]{:S(2)}) %collective-permute-start.1) | collective-permute-done | bytes 720928 | tf_op jit(solution)/shard_map/while/body/eval_jaxpr/ppermute | solution.py:12
  252.1 6.5 %collective-permute-done = bf16[352,1024]{1,0:T(8,128)(2,1)} collective-permute-done((bf16[352,1024]{1,0:T(8,128)(2,1)S(1)}, bf16[352,1024]{1,0:T(8,128)(2,1)}, u32[]{:S(2)}, u32[]{:S(2)}) %collective-permute-start) | collective-permute-done | bytes 720928 | tf_op jit(solution)/shard_map/while/body/eval_jaxpr/ppermute | solution.py:12
  261.2 1.8 fusion.48
  264.2 2.3 convolution_add_fusion.5
  266.6 10.8 %collective-permute-done.1 = bf16[352,1024]{1,0:T(8,128)(2,1)} collective-permute-done((bf16[352,1024]{1,0:T(8,128)(2,1)}, bf16[352,1024]{1,0:T(8,128)(2,1)}, u32[]{:S(2)}, u32[]{:S(2)}) %collective-permute-start.1) | collective-permute-done | bytes 720928 | tf_op jit(solution)/shard_map/while/body/eval_jaxpr/ppermute | solution.py:12
  278.6 6.5 %collective-permute-done = bf16[352,1024]{1,0:T(8,128)(2,1)} collective-permute-done((bf16[352,1024]{1,0:T(8,128)(2,1)S(1)}, bf16[352,1024]{1,0:T(8,128)(2,1)}, u32[]{:S(2)}, u32[]{:S(2)}) %collective-permute-start) | collective-permute-done | bytes 720928 | tf_op jit(solution)/shard_map/while/body/eval_jaxpr/ppermute | solution.py:12
  287.8 1.8 fusion.48
  290.8 2.3 convolution_add_fusion.5
  293.1 10.8 %collective-permute-done.1 = bf16[352,1024]{1,0:T(8,128)(2,1)} collective-permute-done((bf16[352,1024]{1,0:T(8,128)(2,1)}, bf16[352,1024]{1,0:T(8,128)(2,1)}, u32[]{:S(2)}, u32[]{:S(2)}) %collective-permute-start.1) | collective-permute-done | bytes 720928 | tf_op jit(solution)/shard_map/while/body/eval_jaxpr/ppermute | solution.py:12
  305.2 6.5 %collective-permute-done = bf16[352,1024]{1,0:T(8,128)(2,1)} collective-permute-done((bf16[352,1024]{1,0:T(8,128)(2,1)S(1)}, bf16[352,1024]{1,0:T(8,128)(2,1)}, u32[]{:S(2)}, u32[]{:S(2)}) %collective-permute-start) | collective-permute-done | bytes 720928 | tf_op jit(solution)/shard_map/while/body/eval_jaxpr/ppermute | solution.py:12
  317.3 2.3 convolution_add_fusion.5
  319.7 10.8 %collective-permute-done.1 = bf16[352,1024]{1,0:T(8,128)(2,1)} collective-permute-done((bf16[352,1024]{1,0:T(8,128)(2,1)}, bf16[352,1024]{1,0:T(8,128)(2,1)}, u32[]{:S(2)}, u32[]{:S(2)}) %collective-permute-start.1) | collective-permute-done | bytes 720928 | tf_op jit(solution)/shard_map/while/body/eval_jaxpr/ppermute | solution.py:12
  331.7 6.5 %collective-permute-done = bf16[352,1024]{1,0:T(8,128)(2,1)} collective-permute-done((bf16[352,1024]{1,0:T(8,128)(2,1)S(1)}, bf16[352,1024]{1,0:T(8,128)(2,1)}, u32[]{:S(2)}, u32[]{:S(2)}) %collective-permute-start) | collective-permute-done | bytes 720928 | tf_op jit(solution)/shard_map/while/body/eval_jaxpr/ppermute | solution.py:12
  340.9 1.8 fusion.48
  343.9 2.3 convolution_add_fusion.5
  346.2 10.8 %collective-permute-done.1 = bf16[352,1024]{1,0:T(8,128)(2,1)} collective-permute-done((bf16[352,1024]{1,0:T(8,128)(2,1)}, bf16[352,1024]{1,0:T(8,128)(2,1)}, u32[]{:S(2)}, u32[]{:S(2)}) %collective-permute-start.1) | collective-permute-done | bytes 720928 | tf_op jit(solution)/shard_map/while/body/eval_jaxpr/ppermute | solution.py:12
  358.3 6.5 %collective-permute-done = bf16[352,1024]{1,0:T(8,128)(2,1)} collective-permute-done((bf16[352,1024]{1,0:T(8,128)(2,1)S(1)}, bf16[352,1024]{1,0:T(8,128)(2,1)}, u32[]{:S(2)}, u32[]{:S(2)}) %collective-permute-start) | collective-permute-done | bytes 720928 | tf_op jit(solution)/shard_map/while/body/eval_jaxpr/ppermute | solution.py:12
  367.4 1.8 fusion.48
  370.4 2.3 convolution_add_fusion.5
  372.7 10.8 %collective-permute-done.1 = bf16[352,1024]{1,0:T(8,128)(2,1)} collective-permute-done((bf16[352,1024]{1,0:T(8,128)(2,1)}, bf16[352,1024]{1,0:T(8,128)(2,1)}, u32[]{:S(2)}, u32[]{:S(2)}) %collective-permute-start.1) | collective-permute-done | bytes 720928 | tf_op jit(solution)/shard_map/while/body/eval_jaxpr/ppermute | solution.py:12
  384.8 6.5 %collective-permute-done = bf16[352,1024]{1,0:T(8,128)(2,1)} collective-permute-done((bf16[352,1024]{1,0:T(8,128)(2,1)S(1)}, bf16[352,1024]{1,0:T(8,128)(2,1)}, u32[]{:S(2)}, u32[]{:S(2)}) %collective-permute-start) | collective-permute-done | bytes 720928 | tf_op jit(solution)/shard_map/while/body/eval_jaxpr/ppermute | solution.py:12
  393.9 1.8 fusion.48
  397.0 2.3 convolution_add_fusion.5
  399.3 10.8 %collective-permute-done.1 = bf16[352,1024]{1,0:T(8,128)(2,1)} collective-permute-done((bf16[352,1024]{1,0:T(8,128)(2,1)}, bf16[352,1024]{1,0:T(8,128)(2,1)}, u32[]{:S(2)}, u32[]{:S(2)}) %collective-permute-start.1) | collective-permute-done | bytes 720928 | tf_op jit(solution)/shard_map/while/body/eval_jaxpr/ppermute | solution.py:12
  411.4 6.5 %collective-permute-done = bf16[352,1024]{1,0:T(8,128)(2,1)} collective-permute-done((bf16[352,1024]{1,0:T(8,128)(2,1)S(1)}, bf16[352,1024]{1,0:T(8,128)(2,1)}, u32[]{:S(2)}, u32[]{:S(2)}) %collective-permute-start) | collective-permute-done | bytes 720928 | tf_op jit(solution)/shard_map/while/body/eval_jaxpr/ppermute | solution.py:12
  423.5 2.3 convolution_add_fusion.5
  425.8 10.8 %collective-permute-done.1 = bf16[352,1024]{1,0:T(8,128)(2,1)} collective-permute-done((bf16[352,1024]{1,0:T(8,128)(2,1)}, bf16[352,1024]{1,0:T(8,128)(2,1)}, u32[]{:S(2)}, u32[]{:S(2)}) %collective-permute-start.1) | collective-permute-done | bytes 720928 | tf_op jit(solution)/shard_map/while/body/eval_jaxpr/ppermute | solution.py:12
  437.9 6.5 %collective-permute-done = bf16[352,1024]{1,0:T(8,128)(2,1)} collective-permute-done((bf16[352,1024]{1,0:T(8,128)(2,1)S(1)}, bf16[352,1024]{1,0:T(8,128)(2,1)}, u32[]{:S(2)}, u32[]{:S(2)}) %collective-permute-start) | collective-permute-done | bytes 720928 | tf_op jit(solution)/shard_map/while/body/eval_jaxpr/ppermute | solution.py:12
  447.0 1.8 fusion.48
  450.0 2.3 convolution_add_fusion.5
  452.4 10.8 %collective-permute-done.1 = bf16[352,1024]{1,0:T(8,128)(2,1)} collective-permute-done((bf16[352,1024]{1,0:T(8,128)(2,1)}, bf16[352,1024]{1,0:T(8,128)(2,1)}, u32[]{:S(2)}, u32[]{:S(2)}) %collective-permute-start.1) | collective-permute-done | bytes 720928 | tf_op jit(solution)/shard_map/while/body/eval_jaxpr/ppermute | solution.py:12
  464.4 6.5 %collective-permute-done = bf16[352,1024]{1,0:T(8,128)(2,1)} collective-permute-done((bf16[352,1024]{1,0:T(8,128)(2,1)S(1)}, bf16[352,1024]{1,0:T(8,128)(2,1)}, u32[]{:S(2)}, u32[]{:S(2)}) %collective-permute-start) | collective-permute-done | bytes 720928 | tf_op jit(solution)/shard_map/while/body/eval_jaxpr/ppermute | solution.py:12
  473.6 1.8 fusion.48
  476.6 2.3 convolution_add_fusion.5
  478.9 10.8 %collective-permute-done.1 = bf16[352,1024]{1,0:T(8,128)(2,1)} collective-permute-done((bf16[352,1024]{1,0:T(8,128)(2,1)}, bf16[352,1024]{1,0:T(8,128)(2,1)}, u32[]{:S(2)}, u32[]{:S(2)}) %collective-permute-start.1) | collective-permute-done | bytes 720928 | tf_op jit(solution)/shard_map/while/body/eval_jaxpr/ppermute | solution.py:12
  491.0 6.5 %collective-permute-done = bf16[352,1024]{1,0:T(8,128)(2,1)} collective-permute-done((bf16[352,1024]{1,0:T(8,128)(2,1)S(1)}, bf16[352,1024]{1,0:T(8,128)(2,1)}, u32[]{:S(2)}, u32[]{:S(2)}) %collective-permute-start) | collective-permute-done | bytes 720928 | tf_op jit(solution)/shard_map/while/body/eval_jaxpr/ppermute | solution.py:12
  503.1 2.3 convolution_add_fusion.5
  505.5 10.8 %collective-permute-done.1 = bf16[352,1024]{1,0:T(8,128)(2,1)} collective-permute-done((bf16[352,1024]{1,0:T(8,128)(2,1)}, bf16[352,1024]{1,0:T(8,128)(2,1)}, u32[]{:S(2)}, u32[]{:S(2)}) %collective-permute-start.1) | collective-permute-done | bytes 720928 | tf_op jit(solution)/shard_map/while/body/eval_jaxpr/ppermute | solution.py:12
  517.5 6.5 %collective-permute-done = bf16[352,1024]{1,0:T(8,128)(2,1)} collective-permute-done((bf16[352,1024]{1,0:T(8,128)(2,1)S(1)}, bf16[352,1024]{1,0:T(8,128)(2,1)}, u32[]{:S(2)}, u32[]{:S(2)}) %collective-permute-start) | collective-permute-done | bytes 720928 | tf_op jit(solution)/shard_map/while/body/eval_jaxpr/ppermute | solution.py:12
  529.7 2.3 convolution_add_fusion.5
  532.0 10.8 %collective-permute-done.1 = bf16[352,1024]{1,0:T(8,128)(2,1)} collective-permute-done((bf16[352,1024]{1,0:T(8,128)(2,1)}, bf16[352,1024]{1,0:T(8,128)(2,1)}, u32[]{:S(2)}, u32[]{:S(2)}) %collective-permute-start.1) | collective-permute-done | bytes 720928 | tf_op jit(solution)/shard_map/while/body/eval_jaxpr/ppermute | solution.py:12
  544.1 6.5 %collective-permute-done = bf16[352,1024]{1,0:T(8,128)(2,1)} collective-permute-done((bf16[352,1024]{1,0:T(8,128)(2,1)S(1)}, bf16[352,1024]{1,0:T(8,128)(2,1)}, u32[]{:S(2)}, u32[]{:S(2)}) %collective-permute-start) | collective-permute-done | bytes 720928 | tf_op jit(solution)/shard_map/while/body/eval_jaxpr/ppermute | solution.py:12
  561.6 62.6 %reduce-scatter.4.cloned.1.call-done = bf16[128,352]{1,0:T(8,128)(2,1)} async-done(((bf16[1024,352]{1,0:T(8,128)(2,1)}), bf16[128,352]{1,0:T(8,128)(2,1)}) %reduce-scatter.4.cloned.1.call-update) | async-done | bytes 90128
  (177 shorter events, 111.9 us)
Async XLA Ops:
  7.2 114.7 %copy-start = (bf16[352,1024]{1,0:T(8,128)(2,1)S(1)}, bf16[352,1024]{1,0:T(8,128)(2,1)}, u32[]{:S(2)}) copy-start(bf16[352,1024]{1,0:T(8,128)(2,1)} %param.9) | copy-start | bytes 2162692
  7.2 60.1 %all-gather.5.cloned.1.call-start = ((), (), s32[]{:S(2)}) async-start(), calls=%async_computation.2 | async-start | bytes 2359296 | tf_op jit(solution)/shard_map/all_gather | solution.py:65
  7.9 113.9 %all-gather.3.cloned.1.call-start = ((), (), s32[]{:S(2)}) async-start(), calls=%async_computation.1 | async-start | bytes 2359296 | tf_op jit(solution)/shard_map/all_gather | solution.py:64
  8.7 615.5 %reduce-scatter.4.cloned.1.call-start = ((), (), s32[]{:S(2)}) async-start(), calls=%async_computation.3 | async-start | bytes 884736
  69.7 54.8 %copy-start.5 = (f32[176,1024]{1,0:T(8,128)}, f32[176,1024]{1,0:T(8,128)S(1)}, u32[]{:S(2)}) copy-start(f32[176,1024]{1,0:T(8,128)S(1)} %get-tuple-element.336) | copy-start | bytes 2162692
  124.5 1.4 copy-start.2
  131.6 13.1 %collective-permute-start.1 = (bf16[352,1024]{1,0:T(8,128)(2,1)}, bf16[352,1024]{1,0:T(8,128)(2,1)}, u32[]{:S(2)}, u32[]{:S(2)}) collective-permute-start(bf16[352,1024]{1,0:T(8,128)(2,1)} %fusion.49), channel_id=1, source_target_pairs={{0,8},{8,16},{16,24},{24,32},{32,40},{40,48},{48,56},{56,64},{64,7... | collective-permute-start | bytes 2162696 | tf_op jit(solution)/shard_map/while/body/eval_jaxpr/ppermute | solution.py:12
  131.6 20.9 %collective-permute-start = (bf16[352,1024]{1,0:T(8,128)(2,1)S(1)}, bf16[352,1024]{1,0:T(8,128)(2,1)}, u32[]{:S(2)}, u32[]{:S(2)}) collective-permute-start(bf16[352,1024]{1,0:T(8,128)(2,1)S(1)} %copy.16), channel_id=1, source_target_pairs={{0,8},{8,16},{16,24},{24,32},{32,40},{40,48},{48,56},{56,64},{64,7... | collective-permute-start | bytes 2162696 | tf_op jit(solution)/shard_map/while/body/eval_jaxpr/ppermute | solution.py:12
  158.1 13.1 %collective-permute-start.1 = (bf16[352,1024]{1,0:T(8,128)(2,1)}, bf16[352,1024]{1,0:T(8,128)(2,1)}, u32[]{:S(2)}, u32[]{:S(2)}) collective-permute-start(bf16[352,1024]{1,0:T(8,128)(2,1)} %fusion.49), channel_id=1, source_target_pairs={{0,8},{8,16},{16,24},{24,32},{32,40},{40,48},{48,56},{56,64},{64,7... | collective-permute-start | bytes 2162696 | tf_op jit(solution)/shard_map/while/body/eval_jaxpr/ppermute | solution.py:12
  158.1 20.9 %collective-permute-start = (bf16[352,1024]{1,0:T(8,128)(2,1)S(1)}, bf16[352,1024]{1,0:T(8,128)(2,1)}, u32[]{:S(2)}, u32[]{:S(2)}) collective-permute-start(bf16[352,1024]{1,0:T(8,128)(2,1)S(1)} %copy.16), channel_id=1, source_target_pairs={{0,8},{8,16},{16,24},{24,32},{32,40},{40,48},{48,56},{56,64},{64,7... | collective-permute-start | bytes 2162696 | tf_op jit(solution)/shard_map/while/body/eval_jaxpr/ppermute | solution.py:12
  184.6 13.1 %collective-permute-start.1 = (bf16[352,1024]{1,0:T(8,128)(2,1)}, bf16[352,1024]{1,0:T(8,128)(2,1)}, u32[]{:S(2)}, u32[]{:S(2)}) collective-permute-start(bf16[352,1024]{1,0:T(8,128)(2,1)} %fusion.49), channel_id=1, source_target_pairs={{0,8},{8,16},{16,24},{24,32},{32,40},{40,48},{48,56},{56,64},{64,7... | collective-permute-start | bytes 2162696 | tf_op jit(solution)/shard_map/while/body/eval_jaxpr/ppermute | solution.py:12
  184.6 20.9 %collective-permute-start = (bf16[352,1024]{1,0:T(8,128)(2,1)S(1)}, bf16[352,1024]{1,0:T(8,128)(2,1)}, u32[]{:S(2)}, u32[]{:S(2)}) collective-permute-start(bf16[352,1024]{1,0:T(8,128)(2,1)S(1)} %copy.16), channel_id=1, source_target_pairs={{0,8},{8,16},{16,24},{24,32},{32,40},{40,48},{48,56},{56,64},{64,7... | collective-permute-start | bytes 2162696 | tf_op jit(solution)/shard_map/while/body/eval_jaxpr/ppermute | solution.py:12
  211.2 13.1 %collective-permute-start.1 = (bf16[352,1024]{1,0:T(8,128)(2,1)}, bf16[352,1024]{1,0:T(8,128)(2,1)}, u32[]{:S(2)}, u32[]{:S(2)}) collective-permute-start(bf16[352,1024]{1,0:T(8,128)(2,1)} %fusion.49), channel_id=1, source_target_pairs={{0,8},{8,16},{16,24},{24,32},{32,40},{40,48},{48,56},{56,64},{64,7... | collective-permute-start | bytes 2162696 | tf_op jit(solution)/shard_map/while/body/eval_jaxpr/ppermute | solution.py:12
  211.2 20.9 %collective-permute-start = (bf16[352,1024]{1,0:T(8,128)(2,1)S(1)}, bf16[352,1024]{1,0:T(8,128)(2,1)}, u32[]{:S(2)}, u32[]{:S(2)}) collective-permute-start(bf16[352,1024]{1,0:T(8,128)(2,1)S(1)} %copy.16), channel_id=1, source_target_pairs={{0,8},{8,16},{16,24},{24,32},{32,40},{40,48},{48,56},{56,64},{64,7... | collective-permute-start | bytes 2162696 | tf_op jit(solution)/shard_map/while/body/eval_jaxpr/ppermute | solution.py:12
  237.7 13.1 %collective-permute-start.1 = (bf16[352,1024]{1,0:T(8,128)(2,1)}, bf16[352,1024]{1,0:T(8,128)(2,1)}, u32[]{:S(2)}, u32[]{:S(2)}) collective-permute-start(bf16[352,1024]{1,0:T(8,128)(2,1)} %fusion.49), channel_id=1, source_target_pairs={{0,8},{8,16},{16,24},{24,32},{32,40},{40,48},{48,56},{56,64},{64,7... | collective-permute-start | bytes 2162696 | tf_op jit(solution)/shard_map/while/body/eval_jaxpr/ppermute | solution.py:12
  237.7 20.9 %collective-permute-start = (bf16[352,1024]{1,0:T(8,128)(2,1)S(1)}, bf16[352,1024]{1,0:T(8,128)(2,1)}, u32[]{:S(2)}, u32[]{:S(2)}) collective-permute-start(bf16[352,1024]{1,0:T(8,128)(2,1)S(1)} %copy.16), channel_id=1, source_target_pairs={{0,8},{8,16},{16,24},{24,32},{32,40},{40,48},{48,56},{56,64},{64,7... | collective-permute-start | bytes 2162696 | tf_op jit(solution)/shard_map/while/body/eval_jaxpr/ppermute | solution.py:12
  264.2 13.1 %collective-permute-start.1 = (bf16[352,1024]{1,0:T(8,128)(2,1)}, bf16[352,1024]{1,0:T(8,128)(2,1)}, u32[]{:S(2)}, u32[]{:S(2)}) collective-permute-start(bf16[352,1024]{1,0:T(8,128)(2,1)} %fusion.49), channel_id=1, source_target_pairs={{0,8},{8,16},{16,24},{24,32},{32,40},{40,48},{48,56},{56,64},{64,7... | collective-permute-start | bytes 2162696 | tf_op jit(solution)/shard_map/while/body/eval_jaxpr/ppermute | solution.py:12
  264.2 20.9 %collective-permute-start = (bf16[352,1024]{1,0:T(8,128)(2,1)S(1)}, bf16[352,1024]{1,0:T(8,128)(2,1)}, u32[]{:S(2)}, u32[]{:S(2)}) collective-permute-start(bf16[352,1024]{1,0:T(8,128)(2,1)S(1)} %copy.16), channel_id=1, source_target_pairs={{0,8},{8,16},{16,24},{24,32},{32,40},{40,48},{48,56},{56,64},{64,7... | collective-permute-start | bytes 2162696 | tf_op jit(solution)/shard_map/while/body/eval_jaxpr/ppermute | solution.py:12
  290.8 13.1 %collective-permute-start.1 = (bf16[352,1024]{1,0:T(8,128)(2,1)}, bf16[352,1024]{1,0:T(8,128)(2,1)}, u32[]{:S(2)}, u32[]{:S(2)}) collective-permute-start(bf16[352,1024]{1,0:T(8,128)(2,1)} %fusion.49), channel_id=1, source_target_pairs={{0,8},{8,16},{16,24},{24,32},{32,40},{40,48},{48,56},{56,64},{64,7... | collective-permute-start | bytes 2162696 | tf_op jit(solution)/shard_map/while/body/eval_jaxpr/ppermute | solution.py:12
  290.8 20.9 %collective-permute-start = (bf16[352,1024]{1,0:T(8,128)(2,1)S(1)}, bf16[352,1024]{1,0:T(8,128)(2,1)}, u32[]{:S(2)}, u32[]{:S(2)}) collective-permute-start(bf16[352,1024]{1,0:T(8,128)(2,1)S(1)} %copy.16), channel_id=1, source_target_pairs={{0,8},{8,16},{16,24},{24,32},{32,40},{40,48},{48,56},{56,64},{64,7... | collective-permute-start | bytes 2162696 | tf_op jit(solution)/shard_map/while/body/eval_jaxpr/ppermute | solution.py:12
  317.3 13.1 %collective-permute-start.1 = (bf16[352,1024]{1,0:T(8,128)(2,1)}, bf16[352,1024]{1,0:T(8,128)(2,1)}, u32[]{:S(2)}, u32[]{:S(2)}) collective-permute-start(bf16[352,1024]{1,0:T(8,128)(2,1)} %fusion.49), channel_id=1, source_target_pairs={{0,8},{8,16},{16,24},{24,32},{32,40},{40,48},{48,56},{56,64},{64,7... | collective-permute-start | bytes 2162696 | tf_op jit(solution)/shard_map/while/body/eval_jaxpr/ppermute | solution.py:12
  317.3 20.9 %collective-permute-start = (bf16[352,1024]{1,0:T(8,128)(2,1)S(1)}, bf16[352,1024]{1,0:T(8,128)(2,1)}, u32[]{:S(2)}, u32[]{:S(2)}) collective-permute-start(bf16[352,1024]{1,0:T(8,128)(2,1)S(1)} %copy.16), channel_id=1, source_target_pairs={{0,8},{8,16},{16,24},{24,32},{32,40},{40,48},{48,56},{56,64},{64,7... | collective-permute-start | bytes 2162696 | tf_op jit(solution)/shard_map/while/body/eval_jaxpr/ppermute | solution.py:12
  343.9 13.1 %collective-permute-start.1 = (bf16[352,1024]{1,0:T(8,128)(2,1)}, bf16[352,1024]{1,0:T(8,128)(2,1)}, u32[]{:S(2)}, u32[]{:S(2)}) collective-permute-start(bf16[352,1024]{1,0:T(8,128)(2,1)} %fusion.49), channel_id=1, source_target_pairs={{0,8},{8,16},{16,24},{24,32},{32,40},{40,48},{48,56},{56,64},{64,7... | collective-permute-start | bytes 2162696 | tf_op jit(solution)/shard_map/while/body/eval_jaxpr/ppermute | solution.py:12
  343.9 20.9 %collective-permute-start = (bf16[352,1024]{1,0:T(8,128)(2,1)S(1)}, bf16[352,1024]{1,0:T(8,128)(2,1)}, u32[]{:S(2)}, u32[]{:S(2)}) collective-permute-start(bf16[352,1024]{1,0:T(8,128)(2,1)S(1)} %copy.16), channel_id=1, source_target_pairs={{0,8},{8,16},{16,24},{24,32},{32,40},{40,48},{48,56},{56,64},{64,7... | collective-permute-start | bytes 2162696 | tf_op jit(solution)/shard_map/while/body/eval_jaxpr/ppermute | solution.py:12
  370.4 13.1 %collective-permute-start.1 = (bf16[352,1024]{1,0:T(8,128)(2,1)}, bf16[352,1024]{1,0:T(8,128)(2,1)}, u32[]{:S(2)}, u32[]{:S(2)}) collective-permute-start(bf16[352,1024]{1,0:T(8,128)(2,1)} %fusion.49), channel_id=1, source_target_pairs={{0,8},{8,16},{16,24},{24,32},{32,40},{40,48},{48,56},{56,64},{64,7... | collective-permute-start | bytes 2162696 | tf_op jit(solution)/shard_map/while/body/eval_jaxpr/ppermute | solution.py:12
  370.4 20.9 %collective-permute-start = (bf16[352,1024]{1,0:T(8,128)(2,1)S(1)}, bf16[352,1024]{1,0:T(8,128)(2,1)}, u32[]{:S(2)}, u32[]{:S(2)}) collective-permute-start(bf16[352,1024]{1,0:T(8,128)(2,1)S(1)} %copy.16), channel_id=1, source_target_pairs={{0,8},{8,16},{16,24},{24,32},{32,40},{40,48},{48,56},{56,64},{64,7... | collective-permute-start | bytes 2162696 | tf_op jit(solution)/shard_map/while/body/eval_jaxpr/ppermute | solution.py:12
  396.9 13.1 %collective-permute-start.1 = (bf16[352,1024]{1,0:T(8,128)(2,1)}, bf16[352,1024]{1,0:T(8,128)(2,1)}, u32[]{:S(2)}, u32[]{:S(2)}) collective-permute-start(bf16[352,1024]{1,0:T(8,128)(2,1)} %fusion.49), channel_id=1, source_target_pairs={{0,8},{8,16},{16,24},{24,32},{32,40},{40,48},{48,56},{56,64},{64,7... | collective-permute-start | bytes 2162696 | tf_op jit(solution)/shard_map/while/body/eval_jaxpr/ppermute | solution.py:12
  397.0 20.9 %collective-permute-start = (bf16[352,1024]{1,0:T(8,128)(2,1)S(1)}, bf16[352,1024]{1,0:T(8,128)(2,1)}, u32[]{:S(2)}, u32[]{:S(2)}) collective-permute-start(bf16[352,1024]{1,0:T(8,128)(2,1)S(1)} %copy.16), channel_id=1, source_target_pairs={{0,8},{8,16},{16,24},{24,32},{32,40},{40,48},{48,56},{56,64},{64,7... | collective-permute-start | bytes 2162696 | tf_op jit(solution)/shard_map/while/body/eval_jaxpr/ppermute | solution.py:12
  423.5 13.1 %collective-permute-start.1 = (bf16[352,1024]{1,0:T(8,128)(2,1)}, bf16[352,1024]{1,0:T(8,128)(2,1)}, u32[]{:S(2)}, u32[]{:S(2)}) collective-permute-start(bf16[352,1024]{1,0:T(8,128)(2,1)} %fusion.49), channel_id=1, source_target_pairs={{0,8},{8,16},{16,24},{24,32},{32,40},{40,48},{48,56},{56,64},{64,7... | collective-permute-start | bytes 2162696 | tf_op jit(solution)/shard_map/while/body/eval_jaxpr/ppermute | solution.py:12
  423.5 20.9 %collective-permute-start = (bf16[352,1024]{1,0:T(8,128)(2,1)S(1)}, bf16[352,1024]{1,0:T(8,128)(2,1)}, u32[]{:S(2)}, u32[]{:S(2)}) collective-permute-start(bf16[352,1024]{1,0:T(8,128)(2,1)S(1)} %copy.16), channel_id=1, source_target_pairs={{0,8},{8,16},{16,24},{24,32},{32,40},{40,48},{48,56},{56,64},{64,7... | collective-permute-start | bytes 2162696 | tf_op jit(solution)/shard_map/while/body/eval_jaxpr/ppermute | solution.py:12
  450.0 13.1 %collective-permute-start.1 = (bf16[352,1024]{1,0:T(8,128)(2,1)}, bf16[352,1024]{1,0:T(8,128)(2,1)}, u32[]{:S(2)}, u32[]{:S(2)}) collective-permute-start(bf16[352,1024]{1,0:T(8,128)(2,1)} %fusion.49), channel_id=1, source_target_pairs={{0,8},{8,16},{16,24},{24,32},{32,40},{40,48},{48,56},{56,64},{64,7... | collective-permute-start | bytes 2162696 | tf_op jit(solution)/shard_map/while/body/eval_jaxpr/ppermute | solution.py:12
  450.0 20.9 %collective-permute-start = (bf16[352,1024]{1,0:T(8,128)(2,1)S(1)}, bf16[352,1024]{1,0:T(8,128)(2,1)}, u32[]{:S(2)}, u32[]{:S(2)}) collective-permute-start(bf16[352,1024]{1,0:T(8,128)(2,1)S(1)} %copy.16), channel_id=1, source_target_pairs={{0,8},{8,16},{16,24},{24,32},{32,40},{40,48},{48,56},{56,64},{64,7... | collective-permute-start | bytes 2162696 | tf_op jit(solution)/shard_map/while/body/eval_jaxpr/ppermute | solution.py:12
  476.6 13.1 %collective-permute-start.1 = (bf16[352,1024]{1,0:T(8,128)(2,1)}, bf16[352,1024]{1,0:T(8,128)(2,1)}, u32[]{:S(2)}, u32[]{:S(2)}) collective-permute-start(bf16[352,1024]{1,0:T(8,128)(2,1)} %fusion.49), channel_id=1, source_target_pairs={{0,8},{8,16},{16,24},{24,32},{32,40},{40,48},{48,56},{56,64},{64,7... | collective-permute-start | bytes 2162696 | tf_op jit(solution)/shard_map/while/body/eval_jaxpr/ppermute | solution.py:12
  476.6 20.9 %collective-permute-start = (bf16[352,1024]{1,0:T(8,128)(2,1)S(1)}, bf16[352,1024]{1,0:T(8,128)(2,1)}, u32[]{:S(2)}, u32[]{:S(2)}) collective-permute-start(bf16[352,1024]{1,0:T(8,128)(2,1)S(1)} %copy.16), channel_id=1, source_target_pairs={{0,8},{8,16},{16,24},{24,32},{32,40},{40,48},{48,56},{56,64},{64,7... | collective-permute-start | bytes 2162696 | tf_op jit(solution)/shard_map/while/body/eval_jaxpr/ppermute | solution.py:12
  503.1 13.1 %collective-permute-start.1 = (bf16[352,1024]{1,0:T(8,128)(2,1)}, bf16[352,1024]{1,0:T(8,128)(2,1)}, u32[]{:S(2)}, u32[]{:S(2)}) collective-permute-start(bf16[352,1024]{1,0:T(8,128)(2,1)} %fusion.49), channel_id=1, source_target_pairs={{0,8},{8,16},{16,24},{24,32},{32,40},{40,48},{48,56},{56,64},{64,7... | collective-permute-start | bytes 2162696 | tf_op jit(solution)/shard_map/while/body/eval_jaxpr/ppermute | solution.py:12
  503.1 20.9 %collective-permute-start = (bf16[352,1024]{1,0:T(8,128)(2,1)S(1)}, bf16[352,1024]{1,0:T(8,128)(2,1)}, u32[]{:S(2)}, u32[]{:S(2)}) collective-permute-start(bf16[352,1024]{1,0:T(8,128)(2,1)S(1)} %copy.16), channel_id=1, source_target_pairs={{0,8},{8,16},{16,24},{24,32},{32,40},{40,48},{48,56},{56,64},{64,7... | collective-permute-start | bytes 2162696 | tf_op jit(solution)/shard_map/while/body/eval_jaxpr/ppermute | solution.py:12
  529.7 13.1 %collective-permute-start.1 = (bf16[352,1024]{1,0:T(8,128)(2,1)}, bf16[352,1024]{1,0:T(8,128)(2,1)}, u32[]{:S(2)}, u32[]{:S(2)}) collective-permute-start(bf16[352,1024]{1,0:T(8,128)(2,1)} %fusion.49), channel_id=1, source_target_pairs={{0,8},{8,16},{16,24},{24,32},{32,40},{40,48},{48,56},{56,64},{64,7... | collective-permute-start | bytes 2162696 | tf_op jit(solution)/shard_map/while/body/eval_jaxpr/ppermute | solution.py:12
  529.7 20.9 %collective-permute-start = (bf16[352,1024]{1,0:T(8,128)(2,1)S(1)}, bf16[352,1024]{1,0:T(8,128)(2,1)}, u32[]{:S(2)}, u32[]{:S(2)}) collective-permute-start(bf16[352,1024]{1,0:T(8,128)(2,1)S(1)} %copy.16), channel_id=1, source_target_pairs={{0,8},{8,16},{16,24},{24,32},{32,40},{40,48},{48,56},{56,64},{64,7... | collective-permute-start | bytes 2162696 | tf_op jit(solution)/shard_map/while/body/eval_jaxpr/ppermute | solution.py:12
  550.5 1.8 copy-start.3
  552.3 1.6 copy-start.7
  555.9 1.2 copy-start.1
  555.9 1.6 copy-start.6
  557.5 1.6 copy-start.4
Sparse Core Ops, SparseCore 0:
  10.2 57.0 all-gather.4
  69.5 52.3 all-gather.2
  557.3 66.8 reduce-scatter.3
where the time goes:
time: 636 us; the launch traced here: 632 us
  waiting for transfers between devices  448 us (70%)
  matrix products  93.8 us (15%)
  other arithmetic  50.7 us (8%)
  local copies, waits for them, and re-layouts  23.7 us (4%)
  between operations  13.9 us (2%)
    ppermute x32, waiting for transfers between devices, passed_along(): return lax.ppermute(value, axis, pairs)  276 us
    unnamed x4, waiting for transfers between devices  64 us
    all_gather x1, waiting for transfers between devices, body(): lax.all_gather(sentence_projector_matrix, 'tensor', axis=1, tiled=True)  56.4 us
    all_gather x1, waiting for transfers between devices, body(): lax.all_gather(picture_projector_matrix, 'tensor', axis=1, tiled=True)  52.2 us
    dot_general x16, matrix products, step(): jnp.einsum('mc,me->ce', pair_factor, block_z, preferred_element_type=jnp....  36.3 us
    dot_general x16, matrix products, image_tile(): jnp.einsum('me,ce->mc', block_z, cap_z, preferred_element_type=jnp.float32)  28.3 us
    convert_element_type x16, other arithmetic, step(): passed_along(carried.astype(jnp.bfloat16), 'dp', 1).astype(carried.dtype)  20.1 us
    dot_general x16, matrix products, step(): jnp.dot(pair_factor, cap_z, preferred_element_type=jnp.float32)  19.8 us
  transfers between devices with their start and end apart: 35, of which 35 were waited for; matrix products, arithmetic and copies ran while one was open for 10% of the time, Pallas kernels for 0%

commit v1 on v0

v1 whole, which is shorter than its diff:
```python
import jax
import jax.numpy as jnp
from jax import lax
from jax.experimental import pallas as pl
from jax.experimental.pallas import tpu as pltpu
from jax.sharding import PartitionSpec as P

EPS = 1e-06
LOG2E = 1.4426950408889634
MESH = pl.DeviceIdType.MESH
BF = jnp.bfloat16
F32 = jnp.float32

D = 1024
IMG = 352
PAD = 384
HALF = 176
CAP = 176
SL = 128
NT = (((1,), (1,)), ((), ()))
TN = (((0,), (0,)), ((), ()))


def mo(v, k):
    return pl.multiple_of(v, k)


def kernel(
    pic,
    sent,
    wp,
    ws,
    counts,
    sharp,
    bias,
    out_img,
    out_cap,
    wcap,
    wimg,
    plane,
    caps,
    coef,
    vecs,
    starts,
    part,
    own_cap,
    raw_cap,
    cap_in,
    cap_mid,
    img_send,
    img_recv,
    gp,
    gq,
    own_p,
    own_q,
    rpy,
    tpy,
    gp2,
    own_p2,
    rpz,
    tpz,
    rqz,
    tqz,
    gq2,
    own_q2,
    rqy,
    tqy,
    send_sem,
    recv_sem,
):
    dp = lax.axis_index("dp")
    tensor = lax.axis_index("tensor")
    c = dp % 2
    x = (dp // 2) % 4
    yl = dp // 8
    yh = tensor // 4
    z = tensor % 4
    y = yh * 2 + yl
    d = 1 - 2 * c

    def dev(x_, y_, z_, c_):
        return ((y_ % 2) * 8 + x_ * 2 + c_, (y_ // 2) * 4 + z_)

    def ring(v, s):
        return (v + 4 + s) % 4

    xf, xb = dev(ring(x, d), y, z, c), dev(ring(x, -d), y, z, c)
    yf, yb = dev(x, ring(y, d), z, c), dev(x, ring(y, -d), z, c)
    zf, zb = dev(x, y, ring(z, d), c), dev(x, y, ring(z, -d), c)
    core = dev(x, y, z, 1 - c)
    ym = dev(x, 3 - y, z, c)

    barrier = pltpu.get_barrier_semaphore()
    for other in (xf, xb, yf, yb, zf, zb, core):
        pl.semaphore_signal(barrier, inc=1, device_id=other, device_id_type=MESH)
    pl.semaphore_wait(barrier, 7)

    copies = []

    def make(src, dst, target):
        i = len(copies)
        copy = pltpu.make_async_remote_copy(
            src_ref=src,
            dst_ref=dst,
            send_sem=send_sem.at[i],
            recv_sem=recv_sem.at[i],
            device_id=target,
            device_id_type=MESH,
        )
        copies.append(copy)
        return copy

    def go(src, dst, target):
        copy = make(src, dst, target)
        copy.start()
        return copy

    hc = mo(c * 512, 512)

    def col(yh_, z_):
        return pl.ds(mo((yh_ * 4 + z_) * SL, SL), SL)

    def head_start(win, full):
        half = win.at[pl.ds(hc, 512)]
        here = full.at[pl.ds(hc, 512), col(yh, z)]
        st = {}
        st["f"] = go(half, here, zf)
        st["b"] = go(half, here, zb)
        st["m"] = go(half, here, ym)
        return st

    def piece(full, yh_, z_):
        return full.at[pl.ds(hc, 512), col(yh_, z_)]

    def same(full, yh_, z_, target):
        ref = piece(full, yh_, z_)
        return go(ref, ref, target)

    def head_mid(full, st):
        st["f"].wait_recv()
        st["ff"] = same(full, yh, ring(z, -d), zf)
        st["cores"] = [same(full, yh, ring(z, -d), core)]
        st["m"].wait_recv()
        st["mf"] = same(full, 1 - yh, z, zf)
        st["mb"] = same(full, 1 - yh, z, zb)
        st["cores"].append(same(full, 1 - yh, z, core))
        st["b"].wait_recv()
        st["cores"].append(same(full, yh, ring(z, d), core))

    def head_late(full, st):
        st["ff"].wait_recv()
        st["cores"].append(same(full, yh, ring(z, 2), core))
        st["mf"].wait_recv()
        st["mff"] = same(full, 1 - yh, ring(z, -d), zf)
        st["cores"].append(same(full, 1 - yh, ring(z, -d), core))
        st["mb"].wait_recv()
        st["cores"].append(same(full, 1 - yh, ring(z, d), core))

    def head_end(full, st):
        st["mff"].wait_recv()
        st["cores"].append(same(full, 1 - yh, ring(z, 2), core))
        for copy in st["cores"]:
            copy.wait_recv()

    cap_head = head_start(ws, wcap)
    wcap[:, col(yh, z)] = ws[...]

    k_own = yl * 2 + c
    zero = jnp.zeros((PAD - IMG, D), BF)
    for k in range(4):
        plane[k * PAD + IMG : (k + 1) * PAD, :] = zero
    plane[pl.ds(mo(k_own * PAD, PAD), IMG), col(yh, z)] = jnp.dot(
        pic[...], wp[...], preferred_element_type=F32
    ).astype(BF)

    def rows(y_, half):
        return pl.ds(mo(((y_ % 2) * 2 + c) * PAD + half * HALF, 16), HALF)

    def p_z(z_, target):
        ref = plane.at[rows(y, 0), col(yh, z_)]
        return go(ref, ref, target)

    def p_y(y_, target):
        ref = plane.at[rows(y_, 0), pl.ds(mo((y_ // 2) * 512, 512), 512)]
        return go(ref, ref, target)

    def q_y(y_, target):
        ref = plane.at[rows(y_, 1), col(y_ // 2, z)]
        return go(ref, ref, target)

    def q_z(z_, target):
        made = []
        for y_ in range(4):
            ref = plane.at[rows(y_, 1), col(y_ // 2, z_)]
            made.append(go(ref, ref, target))
        return made

    pzf, pzb = p_z(z, zf), p_z(z, zb)
    qyf, qyb = q_y(y, yf), q_y(y, yb)
    head_mid(wcap, cap_head)
    pzf.wait_recv()
    pzff = p_z(ring(z, -d), zf)
    qyf.wait_recv()
    qyff = q_y(ring(y, -d), yf)
    head_late(wcap, cap_head)
    pzb.wait_recv()
    pzff.wait_recv()
    pyf, pyb = p_y(y, yf), p_y(y, yb)
    qyb.wait_recv()
    qyff.wait_recv()
    qzf, qzb = q_z(z, zf), q_z(z, zb)
    head_end(wcap, cap_head)

    raw = jnp.dot(sent[...], wcap[...], preferred_element_type=F32)
    raw_cap[...] = raw
    cap_scale = lax.rsqrt(jnp.sum(raw * raw, axis=1, keepdims=True) + EPS)
    caps[0:CAP, :] = (raw * cap_scale).astype(BF)

    def cap_rows(slot):
        return caps.at[slot * CAP : (slot + 1) * CAP]

    cf = go(cap_rows(0), cap_rows(1), xf)
    cb = go(cap_rows(0), cap_rows(2), xb)
    img_head = head_start(wp, wimg)
    wimg[:, col(yh, z)] = wp[...]

    n = counts[...].astype(F32)
    nb = n.astype(BF)
    a = lax.broadcasted_iota(jnp.int32, (IMG, IMG), 0)
    b = lax.broadcasted_iota(jnp.int32, (IMG, IMG), 1)
    upto = jnp.dot(nb, (a < b).astype(F32).astype(BF), preferred_element_type=F32)
    a = lax.broadcasted_iota(jnp.int32, (16, 16), 0)
    b = lax.broadcasted_iota(jnp.int32, (16, 16), 1)
    before = jnp.dot((b < a).astype(F32).astype(BF), nb, preferred_element_type=F32)
    starts[0:16, 0:IMG] = upto + jnp.sum(before, axis=1, keepdims=True)
    starts[0:16, IMG:PAD] = jnp.full((16, PAD - IMG), -1.0, F32)
    starts[16:32, 0:IMG] = n
    starts[16:32, IMG:PAD] = jnp.full((16, PAD - IMG), 1.0, F32)

    pyf.wait_recv()
    pyff = p_y(ring(y, -d), yf)
    for copy in qzf:
        copy.wait_recv()
    qzff = q_z(ring(z, -d), zf)
    pyb.wait_recv()
    for copy in qzb:
        copy.wait_recv()
    pyff.wait_recv()
    for copy in qzff:
        copy.wait_recv()
    swaps = []
    for yl_ in range(2):
        ref = plane.at[pl.ds(mo((yl_ * 2 + c) * PAD, PAD), IMG)]
        swaps.append(go(ref, ref, core))
    head_mid(wimg, img_head)
    for copy in swaps:
        copy.wait_recv()
    head_late(wimg, img_head)

    t = sharp[0]
    shift = bias[0] * LOG2E
    ones = jnp.ones((8, D), BF)
    for yl_ in range(2):
        for c_ in range(2):
            k = yl_ * 2 + c_
            zk = plane[k * PAD : (k + 1) * PAD, :]
            square = lax.dot_general(ones, zk * zk, NT, preferred_element_type=F32)
            scale = t * lax.rsqrt(square[0:1, :] + EPS)
            row = (yl_ * 4 + x) * 2 + c_
            first = starts[pl.ds(row, 1), :]
            num = starts[pl.ds(16 + row, 1), :]
            lanes = slice(c_ * PAD, (c_ + 1) * PAD)
            vecs[yl_, 0:1, lanes] = scale * LOG2E
            vecs[yl_, 1:2, lanes] = scale
            vecs[yl_, 2:3, lanes] = -scale / num
            vecs[yl_, 3:4, lanes] = first
            vecs[yl_, 4:5, lanes] = jnp.where(first < 0.0, -1.0, first + num)

    cf.wait_recv()
    cff = go(cap_rows(1), cap_rows(3), xf)
    t3 = make(part.at[1], cap_in.at[2], xb)
    t1 = make(part.at[3], cap_in.at[0], xf)

    def one_slot(slot, carry):
        @pl.when(slot == 2)
        def _():
            cb.wait_recv()

        @pl.when(slot == 3)
        def _():
            cff.wait_recv()

        step = jnp.where(slot == 1, -d, jnp.where(slot == 2, d, 2 * (slot // 3)))
        there = ((yl * 4 + ring(x, step)) * 2 + c) * 8 + tensor
        r = pl.ds(mo(slot * CAP, CAP), CAP)
        number = (
            there * CAP + lax.broadcasted_iota(jnp.int32, (CAP, 2 * PAD), 0)
        ).astype(F32)
        total = jnp.zeros((CAP, D), F32)
        for yl_ in range(2):
            zy = plane[yl_ * 2 * PAD : (yl_ + 1) * 2 * PAD, :]
            s = lax.dot_general(caps[r, :], zy, NT, preferred_element_type=F32)
            l2 = s * vecs[yl_, 0:1, :] + shift
            inside = (number >= vecs[yl_, 3:4, :]) & (number < vecs[yl_, 4:5, :])
            e = jnp.exp2(jnp.where(inside, l2, -l2))
            w = jnp.where(inside, vecs[yl_, 2:3, :], vecs[yl_, 1:2, :])
            f = (w / (1.0 + e)).astype(BF)
            coef[yl_, r, :] = f
            total = total + jnp.dot(f, zy, preferred_element_type=F32)
        part[slot] = total.astype(BF)

        @pl.when(slot == 0)
        def _():
            own_cap[...] = total

        @pl.when(slot == 1)
        def _():
            t3.start()

        @pl.when(slot == 3)
        def _():
            t1.start()

        return carry

    lax.fori_loop(0, 4, one_slot, 0)
    head_end(wimg, img_head)

    def grad_rows(yl_, c_):
        f = coef[yl_, :, pl.ds(mo(c_ * PAD, PAD), PAD)]
        return lax.dot_general(f, caps[...], TN, preferred_element_type=F32)

    given = []
    for yl_ in range(2):
        img_send[yl_] = grad_rows(yl_, 1 - c)[0:IMG].astype(BF)
        given.append(go(img_send.at[yl_], img_recv.at[yl_], core))

    t1.wait_recv()
    cap_mid[...] = (part[2].astype(F32) + cap_in[0].astype(F32)).astype(BF)
    t2 = go(cap_mid, cap_in.at[1], xf)

    for yl_ in range(2):
        g = grad_rows(yl_, c)[0:IMG]
        given[yl_].wait_recv()
        g = g + img_recv[yl_].astype(F32)
        u = plane[pl.ds(mo((yl_ * 2 + c) * PAD, PAD), IMG), :].astype(F32)
        size = jnp.sum(u * u, axis=1, keepdims=True) + EPS
        along = jnp.sum(u * g, axis=1, keepdims=True)
        back = (g - u * (along / size)).astype(BF)
        grad = lax.dot_general(back, wimg[...], NT, preferred_element_type=F32)
        gp[yl_] = grad[0:HALF].astype(BF)
        for z_ in range(4):
            for yh_ in range(2):
                j = yh_ * 4 + z_
                at = (yh_ * 2 + yl_) * HALF
                gq[z_, at : at + HALF, :] = grad[
                    HALF:IMG, j * SL : (j + 1) * SL
                ].astype(BF)

    def gp_part(y_):
        return gp.at[y_ % 2, :, pl.ds(mo((y_ // 2) * 512, 512), 512)]

    py1 = go(gp_part(ring(y, 2)), rpy.at[0], yf)
    qz1 = go(gq.at[ring(z, 2)], rqz.at[0], zf)
    py3 = go(gp_part(ring(y, -d)), rpy.at[2], yb)
    qz3 = go(gq.at[ring(z, -d)], rqz.at[2], zb)

    def add(*refs):
        total = refs[0].astype(F32)
        for ref in refs[1:]:
            total = total + ref.astype(F32)
        return total

    py1.wait_recv()
    tpy[...] = add(gp_part(ring(y, d))[...], rpy[0]).astype(BF)
    py2 = go(tpy, rpy.at[1], yf)
    qz1.wait_recv()
    tqz[...] = add(gq[ring(z, d)], rqz[0]).astype(BF)
    qz2 = go(tqz, rqz.at[1], zf)

    t2.wait_recv()
    t3.wait_recv()
    g = own_cap[...] + cap_in[1].astype(F32) + cap_in[2].astype(F32)
    raw = raw_cap[...]
    cap_scale = lax.rsqrt(jnp.sum(raw * raw, axis=1, keepdims=True) + EPS)
    u = raw * cap_scale
    along = jnp.sum(u * g, axis=1, keepdims=True)
    back = (cap_scale * (g - u * along)).astype(BF)
    out_cap[...] = lax.dot_general(
        back, wcap[...], NT, preferred_element_type=F32
    ).astype(BF)

    py3.wait_recv()
    py2.wait_recv()
    own = add(gp_part(y)[...], rpy[1], rpy[2])
    for z_ in range(4):
        cut = own[:, z_ * SL : (z_ + 1) * SL]
        own_p2[z_] = cut
        gp2[z_] = cut.astype(BF)
    pz1 = go(gp2.at[ring(z, 2)], rpz.at[0], zf)
    pz3 = go(gp2.at[ring(z, -d)], rpz.at[2], zb)
    qz3.wait_recv()
    qz2.wait_recv()
    own = add(gq[z], rqz[1], rqz[2])
    for y_ in range(4):
        cut = own[y_ * HALF : (y_ + 1) * HALF]
        own_q2[y_] = cut
        gq2[y_] = cut.astype(BF)
    qy1 = go(gq2.at[ring(y, 2)], rqy.at[0], yf)
    qy3 = go(gq2.at[ring(y, -d)], rqy.at[2], yb)
    pz1.wait_recv()
    tpz[...] = (own_p2[ring(z, d)] + rpz[0].astype(F32)).astype(BF)
    pz2 = go(tpz, rpz.at[1], zf)
    qy1.wait_recv()
    tqy[...] = (own_q2[ring(y, d)] + rqy[0].astype(F32)).astype(BF)
    qy2 = go(tqy, rqy.at[1], yf)
    pz3.wait_recv()
    pz2.wait_recv()
    out_img[0:HALF, :] = (own_p2[z] + add(rpz[1], rpz[2])).astype(BF)
    qy3.wait_recv()
    qy2.wait_recv()
    out_img[HALF:IMG, :] = (own_q2[y] + add(rqy[1], rqy[2])).astype(BF)

    for copy in copies:
        copy.wait_send()


COPIES = 96


def body(pic, sent, wp, ws, counts, sharp, bias):
    vm = pl.BlockSpec(memory_space=pltpu.VMEM)
    sm = pl.BlockSpec(memory_space=pltpu.SMEM)
    scratch = [
        ((D, D), BF),
        ((D, D), BF),
        ((4 * PAD, D), BF),
        ((4 * CAP, D), BF),
        ((2, 4 * CAP, 2 * PAD), BF),
        ((2, 8, 2 * PAD), F32),
        ((32, PAD), F32),
        ((4, CAP, D), BF),
        ((CAP, D), F32),
        ((CAP, D), F32),
        ((3, CAP, D), BF),
        ((CAP, D), BF),
        ((2, IMG, D), BF),
        ((2, IMG, D), BF),
        ((2, HALF, D), BF),
        ((4, 4 * HALF, SL), BF),
        ((8, 128), F32),
        ((8, 128), F32),
        ((3, HALF, 512), BF),
        ((HALF, 512), BF),
        ((4, HALF, SL), BF),
        ((4, HALF, SL), F32),
        ((3, HALF, SL), BF),
        ((HALF, SL), BF),
        ((3, 4 * HALF, SL), BF),
        ((4 * HALF, SL), BF),
        ((4, HALF, SL), BF),
        ((4, HALF, SL), F32),
        ((3, HALF, SL), BF),
        ((HALF, SL), BF),
    ]
    return pl.pallas_call(
        kernel,
        out_shape=(
            jax.ShapeDtypeStruct((IMG, SL), BF),
            jax.ShapeDtypeStruct((CAP, D), BF),
        ),
        in_specs=[vm] * 5 + [sm] * 2,
        out_specs=(vm, vm),
        scratch_shapes=[pltpu.VMEM(shape, kind) for shape, kind in scratch]
        + [pltpu.SemaphoreType.DMA((COPIES,)), pltpu.SemaphoreType.DMA((COPIES,))],
        compiler_params=pltpu.CompilerParams(
            collective_id=0, has_side_effects=True, vmem_limit_bytes=56 * 1024 * 1024
        ),
    )(pic, sent, wp, ws, counts.reshape(16, IMG), sharp, bias)


def solution(mesh):
    in_specs = (
        P("dp", None),
        P(("dp", "tensor"), None),
        P(None, "tensor"),
        P(None, "tensor"),
        P(),
        P(),
        P(),
    )
    out_specs = (P("dp", "tensor"), P(("dp", "tensor"), None))
    return jax.shard_map(body, mesh=mesh, in_specs=in_specs, out_specs=out_specs, check_vma=False)
```

time: 636 us -> 85.4 us (0.13)
  waiting for transfers between devices: 448 us -> 0 us
  matrix products: 93.8 us -> 0 us
  Pallas kernels: 0 us -> 78.5 us
  other arithmetic: 50.7 us -> 0 us
  local copies, waits for them, and re-layouts: 23.7 us -> 4.7 us
  between operations: 13.9 us -> 1.93 us
    ppermute x32 -> x0, waiting for transfers between devices: 276 us -> none  [passed_along(): return lax.ppermute(value, axis, pairs)]
    all_gather x2 -> x0, waiting for transfers between devices: 109 us -> none  [the longest x1 56.4 us: body(): lax.all_gather(sentence_projector_matrix, 'tensor', axis=1, tiled=True)]
    dot_general x54 -> x0, matrix products: 93.8 us -> none  [the longest x16 36.3 us: step(): jnp.einsum('mc,me->ce', pair_factor, block_z, preferred_element_type=jnp....]
    pallas_call x0 -> x1, Pallas kernels: none -> 78.5 us  [body(): pl.pallas_call(kernel, out_shape=(jax.ShapeDtypeStruct((IMG, SL), BF), ja...]
    unnamed x4 -> x0, waiting for transfers between devices: 64 us -> none
    convert_element_type x20 -> x0, other arithmetic: 22 us -> none  [the longest x16 20.1 us: step(): passed_along(carried.astype(jnp.bfloat16), 'dp', 1).astype(carried.dtype)]
    while x16 -> x0, local copies, waits for them, and re-layouts: 17.8 us -> none
    add x32 -> x0, other arithmetic: 12.5 us -> none  [the longest x16 12.4 us: scaling_factor(): other_begin_list + sentence_tally_later]
  transfers between devices with their start and end apart: 35 -> 0, of which waited for: 35 -> 0; matrix products, arithmetic and copies ran while one was open for 10% -> 0% of each run, Pallas kernels for 0% -> 0%
where the time goes in v1:
time: 85.4 us; the launch traced here: 85.1 us
  Pallas kernels  78.5 us (92%)
  local copies, waits for them, and re-layouts  4.7 us (6%)
  between operations  1.93 us (2%)
    pallas_call x1, Pallas kernels, body(): pl.pallas_call(kernel, out_shape=(jax.ShapeDtypeStruct((IMG, SL), BF), ja...  78.5 us
    unnamed x2, local copies, waits for them, and re-layouts  3.28 us

profile of v1, /device:TPU:0, one launch (start us, length us, event | category | flops | bytes accessed | tf_op | source)
XLA Modules:
  0.0 85.1 jit_solution(8190980383445180990)
XLA Ops:
  1.9 1.4 %reshape.7.counts = s32[16,352]{1,0:T(8,128)} reshape(s32[5632]{0:T(1024)} %param.11) | data formatting | bytes 45056 | tf_op jit(solution)/shard_map/reshape | solution.py:479
  3.3 78.5 %shard_map.86 = (bf16[352,128]{1,0:T(8,128)(2,1)}, bf16[176,1024]{1,0:T(8,128)(2,1)}) custom-call(bf16[352,1024]{1,0:T(8,128)(2,1)} %pic.1, bf16[176,1024]{1,0:T(8,128)(2,1)} %sent.1, bf16[1024,128]{1,0:T(8,128)(2,1)} %wp.1, bf16[1024,128]{1,0:T(8,128)(2,1)} %ws.1, s32[16,352]{1,0:T(8,128)} %reshape.7.counts, f32[1]{0:T(128)S(6)} %copy.11.sharp, f32[1]{0:T(128)S(6)} %copy.12.bias), custom_call_target="tpu_custom_call" | custom-call | tf_op jit(solution)/shard_map/pallas_call | solution.py:466
  81.8 1.5 %copy.13 = bf16[352,128]{1,0:T(8,128)(2,1)} copy(bf16[352,128]{1,0:T(8,128)(2,1)} %get-tuple-element.4) | data formatting | bytes 180224
  83.3 1.7 %copy.14 = bf16[176,1024]{1,0:T(8,128)(2,1)} copy(bf16[176,1024]{1,0:T(8,128)(2,1)} %get-tuple-element.5) | data formatting | bytes 720896

commit v2 on v1

v2 whole, which is shorter than its diff:
```python
import jax
import jax.numpy as jnp
from jax import lax
from jax.experimental import pallas as pl
from jax.experimental.pallas import tpu as pltpu
from jax.sharding import PartitionSpec as P

EPS = 1e-06
LOG2E = 1.4426950408889634
MESH = pl.DeviceIdType.MESH
BF = jnp.bfloat16
F32 = jnp.float32

D = 1024
IMG = 352
PAD = 384
HALF = 176
CUT = 256
CAP = 176
SL = 128
NT = (((1,), (1,)), ((), ()))
TN = (((0,), (0,)), ((), ()))


def mo(v, k):
    return pl.multiple_of(v, k)


def kernel(
    pic,
    sent,
    wp,
    ws,
    counts,
    sharp,
    bias,
    out_img,
    out_cap,
    pic_v,
    feat,
    wcap,
    wimg,
    plane,
    caps,
    coef,
    vecs,
    starts,
    part,
    own_cap,
    raw_cap,
    cap_in,
    cap_mid,
    img_send,
    img_own,
    img_recv,
    gp,
    gq,
    rpy,
    tpy,
    gp2,
    own_p2,
    rpz,
    rqz,
    tqz,
    gq2,
    own_q2,
    rqy,
    res_img,
    res_cap,
    send_sem,
    recv_sem,
    load_sem,
):
    dp = lax.axis_index("dp")
    tensor = lax.axis_index("tensor")
    c = dp % 2
    x = (dp // 2) % 4
    yl = dp // 8
    yh = tensor // 4
    z = tensor % 4
    y = yh * 2 + yl
    d = 1 - 2 * c

    def dev(x_, y_, z_, c_):
        return ((y_ % 2) * 8 + x_ * 2 + c_, (y_ // 2) * 4 + z_)

    def ring(v, s):
        return (v + 4 + s) % 4

    def col(yh_, z_):
        return pl.ds(mo((yh_ * 4 + z_) * SL, SL), SL)

    xf, xb = dev(ring(x, d), y, z, c), dev(ring(x, -d), y, z, c)
    yf, yb = dev(x, ring(y, d), z, c), dev(x, ring(y, -d), z, c)
    y2 = dev(x, ring(y, 2), z, c)
    zf, zb = dev(x, y, ring(z, d), c), dev(x, y, ring(z, -d), c)
    z2 = dev(x, y, ring(z, 2), c)
    core = dev(x, y, z, 1 - c)
    ym = dev(x, 3 - y, z, c)

    barrier = pltpu.get_barrier_semaphore()
    for other in (xf, xb, yf, yb, y2, zf, zb, z2, core):
        pl.semaphore_signal(barrier, inc=1, device_id=other, device_id_type=MESH)

    def load(i, src, dst):
        copy = pltpu.make_async_copy(src, dst, load_sem.at[i])
        copy.start()
        return copy

    load_pic = load(0, pic, pic_v)
    load_wp = load(1, wp, wimg.at[:, col(yh, z)])
    load_ws = load(2, ws, wcap.at[:, col(yh, z)])
    load_sent = load(3, sent, feat.at[3 * CAP : 4 * CAP])
    pl.semaphore_wait(barrier, 9)

    copies = []

    def make(src, dst, target):
        i = len(copies)
        copy = pltpu.make_async_remote_copy(
            src_ref=src,
            dst_ref=dst,
            send_sem=send_sem.at[i],
            recv_sem=recv_sem.at[i],
            device_id=target,
            device_id_type=MESH,
        )
        copies.append(copy)
        return copy

    def go(src, dst, target):
        copy = make(src, dst, target)
        copy.start()
        return copy

    hc = mo(c * 512, 512)

    def head_start(win, full):
        half = win.at[pl.ds(hc, 512)]
        here = full.at[pl.ds(hc, 512), col(yh, z)]
        st = {}
        st["m"] = go(half, here, ym)
        st["f"] = go(half, here, zf)
        st["b"] = go(half, here, zb)
        return st

    def same(full, yh_, z_, target):
        ref = full.at[pl.ds(hc, 512), col(yh_, z_)]
        return go(ref, ref, target)

    def head_mid(full, st):
        st["f"].wait_recv()
        st["ff"] = same(full, yh, ring(z, -d), zf)
        st["cores"] = [same(full, yh, ring(z, -d), core)]
        st["m"].wait_recv()
        st["mf"] = same(full, 1 - yh, z, zf)
        st["mb"] = same(full, 1 - yh, z, zb)
        st["cores"].append(same(full, 1 - yh, z, core))
        st["b"].wait_recv()
        st["cores"].append(same(full, yh, ring(z, d), core))

    def head_late(full, st):
        st["mf"].wait_recv()
        st["mff"] = same(full, 1 - yh, ring(z, -d), zf)
        st["cores"].append(same(full, 1 - yh, ring(z, -d), core))
        st["ff"].wait_recv()
        st["cores"].append(same(full, yh, ring(z, 2), core))
        st["mb"].wait_recv()
        st["cores"].append(same(full, 1 - yh, ring(z, d), core))

    def head_end(full, st):
        st["mff"].wait_recv()
        st["cores"].append(same(full, 1 - yh, ring(z, 2), core))
        for copy in st["cores"]:
            copy.wait_recv()

    cap_head = head_start(ws, wcap)

    def slot_rows(slot, lo, hi):
        return feat.at[slot * CAP + lo : slot * CAP + hi]

    xf1 = go(sent.at[0:96], slot_rows(1, 0, 96), xf)
    xb1 = go(sent, slot_rows(2, 0, CAP), xb)
    xf2 = go(sent.at[96:CAP], slot_rows(1, 96, CAP), xf)

    k_own = yl * 2 + c
    zero = jnp.zeros((PAD - IMG, D), BF)
    for k in range(4):
        plane[k * PAD + IMG : (k + 1) * PAD, :] = zero
    load_pic.wait()
    load_wp.wait()
    plane[pl.ds(mo(k_own * PAD, PAD), IMG), col(yh, z)] = jnp.dot(
        pic_v[...], wimg[:, col(yh, z)], preferred_element_type=F32
    ).astype(BF)

    def p_rows(y_):
        return pl.ds(mo(((y_ % 2) * 2 + c) * PAD, 16), CUT)

    def q_rows(y_):
        return pl.ds(mo(((y_ % 2) * 2 + c) * PAD + CUT, 16), IMG - CUT)

    def p_z(z_, target):
        ref = plane.at[p_rows(y), col(yh, z_)]
        return go(ref, ref, target)

    def p_y(y_, target):
        ref = plane.at[p_rows(y_), pl.ds(mo((y_ // 2) * 512, 512), 512)]
        return go(ref, ref, target)

    def q_y(y_, target):
        ref = plane.at[q_rows(y_), col(y_ // 2, z)]
        return go(ref, ref, target)

    def q_z(z_, target):
        made = []
        for y_ in range(4):
            ref = plane.at[q_rows(y_), col(y_ // 2, z_)]
            made.append(go(ref, ref, target))
        return made

    pzf, pzb = p_z(z, zf), p_z(z, zb)
    qyf, qyb = q_y(y, yf), q_y(y, yb)
    head_mid(wcap, cap_head)
    pzf.wait_recv()
    pzff = p_z(ring(z, -d), zf)
    qyf.wait_recv()
    qyff = q_y(ring(y, -d), yf)
    xf1.wait_recv()
    xff1 = go(slot_rows(1, 0, 96), slot_rows(0, 0, 96), xf)
    pzb.wait_recv()
    pzff.wait_recv()
    pyf, pyb = p_y(y, yf), p_y(y, yb)
    swaps = [p_y(y, core)]
    head_late(wcap, cap_head)
    qyb.wait_recv()
    qyff.wait_recv()
    qzf, qzb = q_z(z, zf), q_z(z, zb)
    xf2.wait_recv()
    xff2 = go(slot_rows(1, 96, CAP), slot_rows(0, 96, CAP), xf)

    n = counts[...].astype(F32)
    nb = n.astype(BF)
    a = lax.broadcasted_iota(jnp.int32, (128, 128), 0)
    b = lax.broadcasted_iota(jnp.int32, (128, 128), 1)
    upto = jnp.dot(nb, (a < b).astype(F32).astype(BF), preferred_element_type=F32)
    a = lax.broadcasted_iota(jnp.int32, (44, 44), 0)
    b = lax.broadcasted_iota(jnp.int32, (44, 44), 1)
    before = jnp.dot((b < a).astype(F32).astype(BF), nb, preferred_element_type=F32)
    starts[0, 0:44, :] = upto + jnp.sum(before, axis=1, keepdims=True)
    starts[1, 0:44, :] = n
    starts[0, 44:48, :] = jnp.full((4, 128), -1.0, F32)
    starts[1, 44:48, :] = jnp.full((4, 128), 1.0, F32)

    pyf.wait_recv()
    pyff = p_y(ring(y, -d), yf)
    swaps.append(p_y(ring(y, -d), core))
    for copy in qzf:
        copy.wait_recv()
    qzff = q_z(ring(z, -d), zf)
    head_end(wcap, cap_head)
    pyb.wait_recv()
    swaps.append(p_y(ring(y, d), core))
    for copy in qzb:
        copy.wait_recv()
    img_head = head_start(wp, wimg)

    load_ws.wait()
    load_sent.wait()

    def embed(rows):
        raw = jnp.dot(feat[rows, :], wcap[...], preferred_element_type=F32)
        cap_scale = lax.rsqrt(jnp.sum(raw * raw, axis=1, keepdims=True) + EPS)
        caps[rows, :] = (raw * cap_scale).astype(BF)
        return raw

    xb1.wait_recv()
    raw_cap[...] = embed(slice(2 * CAP, 4 * CAP))[CAP : 2 * CAP]
    pyff.wait_recv()
    swaps.append(p_y(ring(y, 2), core))
    for copy in qzff:
        copy.wait_recv()
    for yl_ in range(2):
        ref = plane.at[q_rows(yl_)]
        swaps.append(go(ref, ref, core))
    xff1.wait_recv()
    xff2.wait_recv()
    embed(slice(0, 2 * CAP))
    head_mid(wimg, img_head)
    for copy in swaps:
        copy.wait_recv()

    t = sharp[0]
    shift = bias[0] * LOG2E
    ones = jnp.ones((8, D), BF)
    even = x % 2 == 0

    def block_vec(which, yl_, c_):
        row = (yl_ * 4 + x) * 2 + c_
        q = (row * 11) // 4
        v = jnp.concatenate([starts[which, pl.ds(q + i, 1), :] for i in range(4)], axis=1)
        cuts = [((2 * p + 3 * c_) % 4) * 32 for p in range(2)]
        return jnp.where(even, v[:, cuts[0] : cuts[0] + PAD], v[:, cuts[1] : cuts[1] + PAD])

    for yl_ in range(2):
        for c_ in range(2):
            k = yl_ * 2 + c_
            zk = plane[k * PAD : (k + 1) * PAD, :]
            square = lax.dot_general(ones, zk * zk, NT, preferred_element_type=F32)
            scale = t * lax.rsqrt(square[0:1, :] + EPS)
            first = block_vec(0, yl_, c_)
            num = block_vec(1, yl_, c_)
            lanes = slice(c_ * PAD, (c_ + 1) * PAD)
            vecs[yl_, 0:1, lanes] = scale * LOG2E
            vecs[yl_, 1:2, lanes] = scale
            vecs[yl_, 2:3, lanes] = -scale / num
            vecs[yl_, 3:4, lanes] = first
            vecs[yl_, 4:5, lanes] = first + num

    t1 = make(part.at[0], cap_in.at[0], xf)
    t3 = make(part.at[1], cap_in.at[2], xb)

    def base(step):
        return (((yl * 4 + ring(x, step)) * 2 + c) * 8 + tensor) * CAP

    def two_slots(g, carry):
        low = jnp.where(g == 0, base(2), base(d))
        high = jnp.where(g == 0, base(-d), base(0))
        i = lax.broadcasted_iota(jnp.int32, (2 * CAP, 1), 0)
        number = (i + jnp.where(i < CAP, low, high - CAP)).astype(F32)
        r = pl.ds(mo(g * 2 * CAP, 2 * CAP), 2 * CAP)
        total = None
        for yl_ in range(2):
            zy = plane[yl_ * 2 * PAD : (yl_ + 1) * 2 * PAD, :]
            s = lax.dot_general(caps[r, :], zy, NT, preferred_element_type=F32)
            l2 = s * vecs[yl_, 0:1, :] + shift
            inside = (number >= vecs[yl_, 3:4, :]) & (number < vecs[yl_, 4:5, :])
            e = jnp.exp2(jnp.where(inside, l2, -l2))
            w = jnp.where(inside, vecs[yl_, 2:3, :], vecs[yl_, 1:2, :])
            f = (w / (1.0 + e)).astype(BF)
            coef[yl_, r, :] = f
            more = jnp.dot(f, zy, preferred_element_type=F32)
            total = more if total is None else total + more
        part[2 * g] = total[0:CAP].astype(BF)
        part[2 * g + 1] = total[CAP : 2 * CAP].astype(BF)

        @pl.when(g == 0)
        def _():
            t1.start()
            t3.start()

        @pl.when(g == 1)
        def _():
            own_cap[...] = total[CAP : 2 * CAP]

        return carry

    lax.fori_loop(0, 2, two_slots, 0)
    head_late(wimg, img_head)

    def grad_rows(yl_, c_):
        f = coef[yl_, :, pl.ds(mo(c_ * PAD, PAD), PAD)]
        return lax.dot_general(f, caps[...], TN, preferred_element_type=F32)

    given = []
    for i, yl_ in enumerate((yl, 1 - yl)):
        img_send[i] = grad_rows(yl_, 1 - c)[0:IMG].astype(BF)
        given.append(go(img_send.at[i], img_recv.at[i], core))
        if i == 0:
            img_own[0] = grad_rows(yl_, c)[0:IMG]
    img_own[1] = grad_rows(1 - yl, c)[0:IMG]
    t1.wait_recv()
    cap_mid[...] = (part[2].astype(F32) + cap_in[0].astype(F32)).astype(BF)
    t2 = go(cap_mid, cap_in.at[1], xf)
    head_end(wimg, img_head)

    def gp_part(y_):
        return gp.at[y_ % 2, :, pl.ds(mo((y_ // 2) * 512, 512), 512)]

    def image_back(i, yl_):
        given[i].wait_recv()
        g = img_own[i] + img_recv[i].astype(F32)
        u = plane[pl.ds(mo((yl_ * 2 + c) * PAD, PAD), IMG), :].astype(F32)
        size = jnp.sum(u * u, axis=1, keepdims=True) + EPS
        along = jnp.sum(u * g, axis=1, keepdims=True)
        back = (g - u * (along / size)).astype(BF)
        grad = lax.dot_general(back, wimg[...], NT, preferred_element_type=F32)
        gp[yl_] = grad[0:HALF].astype(BF)
        for z_ in range(4):
            for yh_ in range(2):
                j = yh_ * 4 + z_
                gq[z_, i, yh_ * HALF : (yh_ + 1) * HALF, :] = grad[
                    HALF:IMG, j * SL : (j + 1) * SL
                ].astype(BF)

    def add(*refs):
        total = refs[0].astype(F32)
        for ref in refs[1:]:
            total = total + ref.astype(F32)
        return total

    image_back(0, yl)
    py1 = go(gp_part(ring(y, 2)), rpy.at[0], yf)
    qz1 = [go(gq.at[ring(z, 2), 0], rqz.at[0, 0], zf)]
    qz3 = [go(gq.at[ring(z, -d), 0], rqz.at[2, 0], zb)]
    image_back(1, 1 - yl)
    py3 = go(gp_part(ring(y, -d)), rpy.at[2], yb)
    qz1.append(go(gq.at[ring(z, 2), 1], rqz.at[0, 1], zf))
    qz3.append(go(gq.at[ring(z, -d), 1], rqz.at[2, 1], zb))
    py1.wait_recv()
    tpy[...] = add(gp_part(ring(y, d))[...], rpy[0]).astype(BF)
    py2 = go(tpy, rpy.at[1], yf)
    qz2 = []
    for i in range(2):
        qz1[i].wait_recv()
        tqz[i] = add(gq[ring(z, d), i], rqz[0, i]).astype(BF)
        qz2.append(go(tqz.at[i], rqz.at[1, i], zf))

    t2.wait_recv()
    t3.wait_recv()
    g = own_cap[...] + cap_in[1].astype(F32) + cap_in[2].astype(F32)
    raw = raw_cap[...]
    cap_scale = lax.rsqrt(jnp.sum(raw * raw, axis=1, keepdims=True) + EPS)
    u = raw * cap_scale
    along = jnp.sum(u * g, axis=1, keepdims=True)
    back = (cap_scale * (g - u * along)).astype(BF)
    res_cap[...] = lax.dot_general(
        back, wcap[...], NT, preferred_element_type=F32
    ).astype(BF)
    store_cap = load(4, res_cap, out_cap)

    py3.wait_recv()
    py2.wait_recv()
    own = add(gp_part(y)[...], rpy[1], rpy[2])
    for z_ in range(4):
        cut = own[:, z_ * SL : (z_ + 1) * SL]
        own_p2[z_] = cut
        gp2[z_] = cut.astype(BF)
    pz = [
        go(gp2.at[ring(z, 2)], rpz.at[0], z2),
        go(gp2.at[ring(z, d)], rpz.at[1], zf),
        go(gp2.at[ring(z, -d)], rpz.at[2], zb),
    ]
    for i in range(2):
        qz3[i].wait_recv()
        qz2[i].wait_recv()
        own = add(gq[z, i], rqz[1, i], rqz[2, i])
        for yh_ in range(2):
            cut = own[yh_ * HALF : (yh_ + 1) * HALF]
            own_q2[i, yh_] = cut
            gq2[i, yh_] = cut.astype(BF)

    def q2(ref, y_):
        return ref.at[(y_ + y) % 2, y_ // 2]

    qy = [
        go(q2(gq2, ring(y, 2)), rqy.at[0], y2),
        go(q2(gq2, ring(y, d)), rqy.at[1], yf),
        go(q2(gq2, ring(y, -d)), rqy.at[2], yb),
    ]
    for copy in pz:
        copy.wait_recv()
    res_img[0:HALF, :] = (own_p2[z] + add(rpz[0], rpz[1], rpz[2])).astype(BF)
    for copy in qy:
        copy.wait_recv()
    res_img[HALF:IMG, :] = (own_q2[0, yh] + add(rqy[0], rqy[1], rqy[2])).astype(BF)
    store_img = load(5, res_img, out_img)
    for copy in copies:
        copy.wait_send()
    store_cap.wait()
    store_img.wait()


def finish(img, cap, out_img, out_cap):
    out_img[...] = img[...]
    out_cap[...] = cap[...]


COPIES = 96


def body(pic, sent, wp, ws, counts, sharp, bias):
    vm = pl.BlockSpec(memory_space=pltpu.VMEM)
    sm = pl.BlockSpec(memory_space=pltpu.SMEM)
    hbm = pl.BlockSpec(memory_space=pl.ANY)
    scratch = [
        ((IMG, D), BF),
        ((4 * CAP, D), BF),
        ((D, D), BF),
        ((D, D), BF),
        ((4 * PAD, D), BF),
        ((4 * CAP, D), BF),
        ((2, 4 * CAP, 2 * PAD), BF),
        ((2, 8, 2 * PAD), F32),
        ((2, 48, 128), F32),
        ((4, CAP, D), BF),
        ((CAP, D), F32),
        ((CAP, D), F32),
        ((3, CAP, D), BF),
        ((CAP, D), BF),
        ((2, IMG, D), BF),
        ((2, IMG, D), F32),
        ((2, IMG, D), BF),
        ((2, HALF, D), BF),
        ((4, 2, 2 * HALF, SL), BF),
        ((3, HALF, 512), BF),
        ((HALF, 512), BF),
        ((4, HALF, SL), BF),
        ((4, HALF, SL), F32),
        ((3, HALF, SL), BF),
        ((3, 2, 2 * HALF, SL), BF),
        ((2, 2 * HALF, SL), BF),
        ((2, 2, HALF, SL), BF),
        ((2, 2, HALF, SL), F32),
        ((3, HALF, SL), BF),
        ((IMG, SL), BF),
        ((CAP, D), BF),
    ]
    outs = (
        jax.ShapeDtypeStruct((IMG, SL), BF),
        jax.ShapeDtypeStruct((CAP, D), BF),
    )
    img, cap = pl.pallas_call(
        kernel,
        out_shape=outs,
        in_specs=[hbm] * 4 + [vm] + [sm] * 2,
        out_specs=(hbm, hbm),
        scratch_shapes=[pltpu.VMEM(shape, kind) for shape, kind in scratch]
        + [
            pltpu.SemaphoreType.DMA((COPIES,)),
            pltpu.SemaphoreType.DMA((COPIES,)),
            pltpu.SemaphoreType.DMA((6,)),
        ],
        compiler_params=pltpu.CompilerParams(
            collective_id=0, has_side_effects=True, vmem_limit_bytes=58 * 1024 * 1024
        ),
    )(pic, sent, wp, ws, counts.reshape(44, 128), sharp, bias)
    return pl.pallas_call(
        finish, out_shape=outs, in_specs=[vm, vm], out_specs=(vm, vm)
    )(img, cap)


def solution(mesh):
    in_specs = (
        P("dp", None),
        P(("dp", "tensor"), None),
        P(None, "tensor"),
        P(None, "tensor"),
        P(),
        P(),
        P(),
    )
    out_specs = (P("dp", "tensor"), P(("dp", "tensor"), None))
    return jax.shard_map(body, mesh=mesh, in_specs=in_specs, out_specs=out_specs, check_vma=False)
```

time: 85.4 us -> 72.6 us (0.85)
  the two profiles are of different devices: /device:TPU:0 before, /device:TPU:2 now
where the time goes in v2:
time: 72.6 us; the launch traced here: 72.4 us
  Pallas kernels  70.5 us (97%)
  between operations  1.93 us (3%)
    pallas_call x1, Pallas kernels, body(): pl.pallas_call(kernel, out_shape=outs, in_specs=[hbm] * 4 + [vm] + [sm] *...  68.7 us
    pallas_call x1, Pallas kernels, body(): pl.pallas_call(finish, out_shape=outs, in_specs=[vm, vm], out_specs=(vm,...  1.81 us

profile of v2, /device:TPU:2, one launch (start us, length us, event | category | flops | bytes accessed | tf_op | source)
XLA Modules:
  0.0 72.4 jit_solution(16059016845912674405)
XLA Ops:
  1.9 68.7 %shard_map.86 = (bf16[352,128]{1,0:T(8,128)(2,1)}, bf16[176,1024]{1,0:T(8,128)(2,1)}) custom-call(bf16[352,1024]{1,0:T(8,128)(2,1)} %pic.1, bf16[176,1024]{1,0:T(8,128)(2,1)} %sent.1, bf16[1024,128]{1,0:T(8,128)(2,1)} %wp.1, bf16[1024,128]{1,0:T(8,128)(2,1)} %ws.1, s32[44,128]{1,0:T(8,128)} %bitcast.1, f32[1]{0:T(128)S(6)} %copy.9.sharp, f32[1]{0:T(128)S(6)} %copy.10.bias), custom_call_target="tpu_custom_call" | custom-call | tf_op jit(solution)/shard_map/pallas_call | solution.py:522
  70.6 1.8 %shard_map.87 = (bf16[352,128]{1,0:T(8,128)(2,1)}, bf16[176,1024]{1,0:T(8,128)(2,1)}) custom-call(bf16[352,128]{1,0:T(8,128)(2,1)} %get-tuple-element.4.img, bf16[176,1024]{1,0:T(8,128)(2,1)} %get-tuple-element.5.cap), custom_call_target="tpu_custom_call" | custom-call | tf_op jit(solution)/shard_map/pallas_call | solution.py:537

commit v3 on v2

--- a/solution.py
+++ b/solution.py
@@ -111,7 +111,6 @@
     load_wp = load(1, wp, wimg.at[:, col(yh, z)])
     load_ws = load(2, ws, wcap.at[:, col(yh, z)])
     load_sent = load(3, sent, feat.at[3 * CAP : 4 * CAP])
-    pl.semaphore_wait(barrier, 9)
 
     copies = []
 
@@ -133,68 +132,19 @@
         copy.start()
         return copy
 
-    hc = mo(c * 512, 512)
-
-    def head_start(win, full):
-        half = win.at[pl.ds(hc, 512)]
-        here = full.at[pl.ds(hc, 512), col(yh, z)]
-        st = {}
-        st["m"] = go(half, here, ym)
-        st["f"] = go(half, here, zf)
-        st["b"] = go(half, here, zb)
-        return st
-
-    def same(full, yh_, z_, target):
-        ref = full.at[pl.ds(hc, 512), col(yh_, z_)]
-        return go(ref, ref, target)
-
-    def head_mid(full, st):
-        st["f"].wait_recv()
-        st["ff"] = same(full, yh, ring(z, -d), zf)
-        st["cores"] = [same(full, yh, ring(z, -d), core)]
-        st["m"].wait_recv()
-        st["mf"] = same(full, 1 - yh, z, zf)
-        st["mb"] = same(full, 1 - yh, z, zb)
-        st["cores"].append(same(full, 1 - yh, z, core))
-        st["b"].wait_recv()
-        st["cores"].append(same(full, yh, ring(z, d), core))
-
-    def head_late(full, st):
-        st["mf"].wait_recv()
-        st["mff"] = same(full, 1 - yh, ring(z, -d), zf)
-        st["cores"].append(same(full, 1 - yh, ring(z, -d), core))
-        st["ff"].wait_recv()
-        st["cores"].append(same(full, yh, ring(z, 2), core))
-        st["mb"].wait_recv()
-        st["cores"].append(same(full, 1 - yh, ring(z, d), core))
-
-    def head_end(full, st):
-        st["mff"].wait_recv()
-        st["cores"].append(same(full, 1 - yh, ring(z, 2), core))
-        for copy in st["cores"]:
-            copy.wait_recv()
-
-    cap_head = head_start(ws, wcap)
-
-    def slot_rows(slot, lo, hi):
-        return feat.at[slot * CAP + lo : slot * CAP + hi]
-
-    xf1 = go(sent.at[0:96], slot_rows(1, 0, 96), xf)
-    xb1 = go(sent, slot_rows(2, 0, CAP), xb)
-    xf2 = go(sent.at[96:CAP], slot_rows(1, 96, CAP), xf)
-
     k_own = yl * 2 + c
     zero = jnp.zeros((PAD - IMG, D), BF)
     for k in range(4):
         plane[k * PAD + IMG : (k + 1) * PAD, :] = zero
+    load_wp.wait()
     load_pic.wait()
-    load_wp.wait()
     plane[pl.ds(mo(k_own * PAD, PAD), IMG), col(yh, z)] = jnp.dot(
         pic_v[...], wimg[:, col(yh, z)], preferred_element_type=F32
     ).astype(BF)
-
-    def p_rows(y_):
-        return pl.ds(mo(((y_ % 2) * 2 + c) * PAD, 16), CUT)
+    pl.semaphore_wait(barrier, 9)
+
+    def p_rows(y_, lo=0, num=CUT):
+        return pl.ds(mo(((y_ % 2) * 2 + c) * PAD + lo, 16), num)
 
     def q_rows(y_):
         return pl.ds(mo(((y_ % 2) * 2 + c) * PAD + CUT, 16), IMG - CUT)
@@ -203,8 +153,8 @@
         ref = plane.at[p_rows(y), col(yh, z_)]
         return go(ref, ref, target)
 
-    def p_y(y_, target):
-        ref = plane.at[p_rows(y_), pl.ds(mo((y_ // 2) * 512, 512), 512)]
+    def p_y(y_, target, lo=0, num=CUT):
+        ref = plane.at[p_rows(y_, lo, num), pl.ds(mo((y_ // 2) * 512, 512), 512)]
         return go(ref, ref, target)
 
     def q_y(y_, target):
@@ -218,25 +168,63 @@
             made.append(go(ref, ref, target))
         return made
 
-    pzf, pzb = p_z(z, zf), p_z(z, zb)
-    qyf, qyb = q_y(y, yf), q_y(y, yb)
-    head_mid(wcap, cap_head)
-    pzf.wait_recv()
-    pzff = p_z(ring(z, -d), zf)
-    qyf.wait_recv()
-    qyff = q_y(ring(y, -d), yf)
+    hc = mo(c * 512, 512)
+
+    def head_start(win, full, straight):
+        half = win.at[pl.ds(hc, 512)]
+        here = full.at[pl.ds(hc, 512), col(yh, z)]
+        st = {"m": go(half, here, ym), "f": go(half, here, zf), "b": go(half, here, zb)}
+        if straight:
+            st["2"] = go(half, here, z2)
+        return st
+
+    def same(full, yh_, z_, target, start=True):
+        ref = full.at[pl.ds(hc, 512), col(yh_, z_)]
+        return (go if start else make)(ref, ref, target)
+
+    def slot_rows(slot, lo, hi):
+        return feat.at[slot * CAP + lo : slot * CAP + hi]
+
+    pz = [p_z(z, target) for target in (zf, zb, z2)]
+    qy = [q_y(y, target) for target in (yf, yb, y2)]
+    head = head_start(ws, wcap, False)
+    xf1 = go(sent.at[0:96], slot_rows(1, 0, 96), xf)
+    xb1 = go(sent, slot_rows(2, 0, CAP), xb)
+    xf2 = go(sent.at[96:CAP], slot_rows(1, 96, CAP), xf)
+
+    for copy in qy:
+        copy.wait_recv()
+    qzf, qzb = q_z(z, zf), q_z(z, zb)
+    for copy in pz:
+        copy.wait_recv()
+    pyf0 = p_y(y, yf, 0, CUT // 2)
+    pyb = p_y(y, yb)
+    pyf1 = p_y(y, yf, CUT // 2, CUT // 2)
+    swaps = [p_y(y, core)]
+    head["m"].wait_recv()
+    head_mf = same(wcap, 1 - yh, z, zf)
+    head_mb = same(wcap, 1 - yh, z, zb)
+    cores = [same(wcap, 1 - yh, z, core)]
+    head["f"].wait_recv()
+    head_ff = same(wcap, yh, ring(z, -d), zf)
+    cores.append(same(wcap, yh, ring(z, -d), core))
     xf1.wait_recv()
     xff1 = go(slot_rows(1, 0, 96), slot_rows(0, 0, 96), xf)
-    pzb.wait_recv()
-    pzff.wait_recv()
-    pyf, pyb = p_y(y, yf), p_y(y, yb)
-    swaps = [p_y(y, core)]
-    head_late(wcap, cap_head)
-    qyb.wait_recv()
-    qyff.wait_recv()
-    qzf, qzb = q_z(z, zf), q_z(z, zb)
+    pyf0.wait_recv()
+    pyff0 = p_y(ring(y, -d), yf, 0, CUT // 2)
+    head["b"].wait_recv()
+    cores.append(same(wcap, yh, ring(z, d), core))
+    for copy in qzf:
+        copy.wait_recv()
+    qzff = q_z(ring(z, -d), zf)
+    head_mf.wait_recv()
+    head_mff = same(wcap, 1 - yh, ring(z, -d), zf)
+    cores.append(same(wcap, 1 - yh, ring(z, -d), core))
     xf2.wait_recv()
     xff2 = go(slot_rows(1, 96, CAP), slot_rows(0, 96, CAP), xf)
+    pyf1.wait_recv()
+    pyff1 = p_y(ring(y, -d), yf, CUT // 2, CUT // 2)
+    swaps.append(p_y(ring(y, -d), core))
 
     n = counts[...].astype(F32)
     nb = n.astype(BF)
@@ -251,18 +239,17 @@
     starts[0, 44:48, :] = jnp.full((4, 128), -1.0, F32)
     starts[1, 44:48, :] = jnp.full((4, 128), 1.0, F32)
 
-    pyf.wait_recv()
-    pyff = p_y(ring(y, -d), yf)
-    swaps.append(p_y(ring(y, -d), core))
-    for copy in qzf:
-        copy.wait_recv()
-    qzff = q_z(ring(z, -d), zf)
-    head_end(wcap, cap_head)
+    head_ff.wait_recv()
+    cores.append(same(wcap, yh, ring(z, 2), core))
+    head_mb.wait_recv()
+    cores.append(same(wcap, 1 - yh, ring(z, d), core))
     pyb.wait_recv()
     swaps.append(p_y(ring(y, d), core))
-    for copy in qzb:
-        copy.wait_recv()
-    img_head = head_start(wp, wimg)
+    head_mff.wait_recv()
+    cores.append(same(wcap, 1 - yh, ring(z, 2), core))
+    ihead = head_start(wp, wimg, True)
+    for copy in cores:
+        copy.wait_recv()
 
     load_ws.wait()
     load_sent.wait()
@@ -275,9 +262,10 @@
 
     xb1.wait_recv()
     raw_cap[...] = embed(slice(2 * CAP, 4 * CAP))[CAP : 2 * CAP]
-    pyff.wait_recv()
+    pyff0.wait_recv()
+    pyff1.wait_recv()
     swaps.append(p_y(ring(y, 2), core))
-    for copy in qzff:
+    for copy in qzb + qzff:
         copy.wait_recv()
     for yl_ in range(2):
         ref = plane.at[q_rows(yl_)]
@@ -285,7 +273,13 @@
     xff1.wait_recv()
     xff2.wait_recv()
     embed(slice(0, 2 * CAP))
-    head_mid(wimg, img_head)
+    ihead["m"].wait_recv()
+    ihead_m = [same(wimg, 1 - yh, z, target) for target in (zf, zb, z2)]
+    icores = [same(wimg, 1 - yh, z, core)]
+    for name, step in (("f", -d), ("b", d), ("2", 2)):
+        ihead[name].wait_recv()
+        icores.append(same(wimg, yh, ring(z, step), core))
+    icores_late = [same(wimg, 1 - yh, ring(z, step), core, False) for step in (-d, d, 2)]
     for copy in swaps:
         copy.wait_recv()
 
@@ -346,16 +340,18 @@
         @pl.when(g == 0)
         def _():
             t1.start()
-            t3.start()
 
         @pl.when(g == 1)
         def _():
             own_cap[...] = total[CAP : 2 * CAP]
+            t3.start()
+            for arrived, copy in zip(ihead_m, icores_late):
+                arrived.wait_recv()
+                copy.start()
 
         return carry
 
     lax.fori_loop(0, 2, two_slots, 0)
-    head_late(wimg, img_head)
 
     def grad_rows(yl_, c_):
         f = coef[yl_, :, pl.ds(mo(c_ * PAD, PAD), PAD)]
@@ -367,11 +363,8 @@
         given.append(go(img_send.at[i], img_recv.at[i], core))
         if i == 0:
             img_own[0] = grad_rows(yl_, c)[0:IMG]
-    img_own[1] = grad_rows(1 - yl, c)[0:IMG]
-    t1.wait_recv()
-    cap_mid[...] = (part[2].astype(F32) + cap_in[0].astype(F32)).astype(BF)
-    t2 = go(cap_mid, cap_in.at[1], xf)
-    head_end(wimg, img_head)
+    for copy in icores + icores_late:
+        copy.wait_recv()
 
     def gp_part(y_):
         return gp.at[y_ % 2, :, pl.ds(mo((y_ // 2) * 512, 512), 512)]
@@ -402,6 +395,10 @@
     py1 = go(gp_part(ring(y, 2)), rpy.at[0], yf)
     qz1 = [go(gq.at[ring(z, 2), 0], rqz.at[0, 0], zf)]
     qz3 = [go(gq.at[ring(z, -d), 0], rqz.at[2, 0], zb)]
+    img_own[1] = grad_rows(1 - yl, c)[0:IMG]
+    t1.wait_recv()
+    cap_mid[...] = (part[2].astype(F32) + cap_in[0].astype(F32)).astype(BF)
+    t2 = go(cap_mid, cap_in.at[1], xf)
     image_back(1, 1 - yl)
     py3 = go(gp_part(ring(y, -d)), rpy.at[2], yb)
     qz1.append(go(gq.at[ring(z, 2), 1], rqz.at[0, 1], zf))

time: 72.6 us -> 66.3 us (0.913)
  the two profiles are of different devices: /device:TPU:2 before, /device:TPU:0 now
where the time goes in v3:
time: 66.3 us; the launch traced here: 66.1 us
  Pallas kernels  64.1 us (97%)
  between operations  1.93 us (3%)
    pallas_call x1, Pallas kernels, body(): pl.pallas_call(kernel, out_shape=outs, in_specs=[hbm] * 4 + [vm] + [sm] *...  62.3 us
    pallas_call x1, Pallas kernels, body(): pl.pallas_call(finish, out_shape=outs, in_specs=[vm, vm], out_specs=(vm,...  1.81 us

profile of v3, /device:TPU:0, one launch (start us, length us, event | category | flops | bytes accessed | tf_op | source)
XLA Modules:
  0.0 66.1 jit_solution(134846881844437123)
XLA Ops:
  1.9 62.3 %shard_map.86 = (bf16[352,128]{1,0:T(8,128)(2,1)}, bf16[176,1024]{1,0:T(8,128)(2,1)}) custom-call(bf16[352,1024]{1,0:T(8,128)(2,1)} %pic.1, bf16[176,1024]{1,0:T(8,128)(2,1)} %sent.1, bf16[1024,128]{1,0:T(8,128)(2,1)} %wp.1, bf16[1024,128]{1,0:T(8,128)(2,1)} %ws.1, s32[44,128]{1,0:T(8,128)} %bitcast.1, f32[1]{0:T(128)S(6)} %copy.9.sharp, f32[1]{0:T(128)S(6)} %copy.10.bias), custom_call_target="tpu_custom_call" | custom-call | tf_op jit(solution)/shard_map/pallas_call | solution.py:519
  64.2 1.8 %shard_map.87 = (bf16[352,128]{1,0:T(8,128)(2,1)}, bf16[176,1024]{1,0:T(8,128)(2,1)}) custom-call(bf16[352,128]{1,0:T(8,128)(2,1)} %get-tuple-element.4.img, bf16[176,1024]{1,0:T(8,128)(2,1)} %get-tuple-element.5.cap), custom_call_target="tpu_custom_call" | custom-call | tf_op jit(solution)/shard_map/pallas_call | solution.py:534

commit v4 on v3

--- a/solution.py
+++ b/solution.py
@@ -37,6 +37,7 @@
     out_img,
     out_cap,
     pic_v,
+    wp_v,
     feat,
     wcap,
     wimg,
@@ -90,6 +91,7 @@
     def col(yh_, z_):
         return pl.ds(mo((yh_ * 4 + z_) * SL, SL), SL)
 
+    x2 = dev(ring(x, 2), y, z, c)
     xf, xb = dev(ring(x, d), y, z, c), dev(ring(x, -d), y, z, c)
     yf, yb = dev(x, ring(y, d), z, c), dev(x, ring(y, -d), z, c)
     y2 = dev(x, ring(y, 2), z, c)
@@ -99,7 +101,7 @@
     ym = dev(x, 3 - y, z, c)
 
     barrier = pltpu.get_barrier_semaphore()
-    for other in (xf, xb, yf, yb, y2, zf, zb, z2, core):
+    for other in (xf, xb, x2, yf, yb, y2, zf, zb, z2, core):
         pl.semaphore_signal(barrier, inc=1, device_id=other, device_id_type=MESH)
 
     def load(i, src, dst):
@@ -108,7 +110,7 @@
         return copy
 
     load_pic = load(0, pic, pic_v)
-    load_wp = load(1, wp, wimg.at[:, col(yh, z)])
+    load_wp = load(1, wp, wp_v)
     load_ws = load(2, ws, wcap.at[:, col(yh, z)])
     load_sent = load(3, sent, feat.at[3 * CAP : 4 * CAP])
 
@@ -132,6 +134,9 @@
         copy.start()
         return copy
 
+    def head_rows(x_):
+        return pl.ds(mo((x_ * 2 + c) * 128, 128), 128)
+
     k_own = yl * 2 + c
     zero = jnp.zeros((PAD - IMG, D), BF)
     for k in range(4):
@@ -139,9 +144,10 @@
     load_wp.wait()
     load_pic.wait()
     plane[pl.ds(mo(k_own * PAD, PAD), IMG), col(yh, z)] = jnp.dot(
-        pic_v[...], wimg[:, col(yh, z)], preferred_element_type=F32
+        pic_v[...], wp_v[...], preferred_element_type=F32
     ).astype(BF)
-    pl.semaphore_wait(barrier, 9)
+    wimg[head_rows(x), col(yh, z)] = wp_v[head_rows(x), :]
+    pl.semaphore_wait(barrier, 10)
 
     def p_rows(y_, lo=0, num=CUT):
         return pl.ds(mo(((y_ % 2) * 2 + c) * PAD + lo, 16), num)
@@ -170,24 +176,28 @@
 
     hc = mo(c * 512, 512)
 
-    def head_start(win, full, straight):
-        half = win.at[pl.ds(hc, 512)]
-        here = full.at[pl.ds(hc, 512), col(yh, z)]
-        st = {"m": go(half, here, ym), "f": go(half, here, zf), "b": go(half, here, zb)}
-        if straight:
-            st["2"] = go(half, here, z2)
-        return st
-
-    def same(full, yh_, z_, target, start=True):
-        ref = full.at[pl.ds(hc, 512), col(yh_, z_)]
+    half = ws.at[pl.ds(hc, 512)]
+    here = wcap.at[pl.ds(hc, 512), col(yh, z)]
+
+    def same(yh_, z_, target):
+        ref = wcap.at[pl.ds(hc, 512), col(yh_, z_)]
+        return go(ref, ref, target)
+
+    def few(yh_, target):
+        ref = wimg.at[head_rows(x), col(yh_, z)]
+        return go(ref, ref, target)
+
+    def many(x_, target, start=True):
+        ref = wimg.at[head_rows(x_)]
         return (go if start else make)(ref, ref, target)
 
     def slot_rows(slot, lo, hi):
         return feat.at[slot * CAP + lo : slot * CAP + hi]
 
+    ihead = [few(yh, target) for target in (ym, zf, zb, z2)]
     pz = [p_z(z, target) for target in (zf, zb, z2)]
     qy = [q_y(y, target) for target in (yf, yb, y2)]
-    head = head_start(ws, wcap, False)
+    head = {"m": go(half, here, ym), "f": go(half, here, zf), "b": go(half, here, zb)}
     xf1 = go(sent.at[0:96], slot_rows(1, 0, 96), xf)
     xb1 = go(sent, slot_rows(2, 0, CAP), xb)
     xf2 = go(sent.at[96:CAP], slot_rows(1, 96, CAP), xf)
@@ -195,6 +205,8 @@
     for copy in qy:
         copy.wait_recv()
     qzf, qzb = q_z(z, zf), q_z(z, zb)
+    ihead[0].wait_recv()
+    ihead += [few(1 - yh, target) for target in (zf, zb, z2)]
     for copy in pz:
         copy.wait_recv()
     pyf0 = p_y(y, yf, 0, CUT // 2)
@@ -202,26 +214,31 @@
     pyf1 = p_y(y, yf, CUT // 2, CUT // 2)
     swaps = [p_y(y, core)]
     head["m"].wait_recv()
-    head_mf = same(wcap, 1 - yh, z, zf)
-    head_mb = same(wcap, 1 - yh, z, zb)
-    cores = [same(wcap, 1 - yh, z, core)]
+    head_mf = same(1 - yh, z, zf)
+    head_mb = same(1 - yh, z, zb)
+    cores = [same(1 - yh, z, core)]
     head["f"].wait_recv()
-    head_ff = same(wcap, yh, ring(z, -d), zf)
-    cores.append(same(wcap, yh, ring(z, -d), core))
+    head_ff = same(yh, ring(z, -d), zf)
+    cores.append(same(yh, ring(z, -d), core))
     xf1.wait_recv()
     xff1 = go(slot_rows(1, 0, 96), slot_rows(0, 0, 96), xf)
     pyf0.wait_recv()
     pyff0 = p_y(ring(y, -d), yf, 0, CUT // 2)
     head["b"].wait_recv()
-    cores.append(same(wcap, yh, ring(z, d), core))
+    cores.append(same(yh, ring(z, d), core))
     for copy in qzf:
         copy.wait_recv()
     qzff = q_z(ring(z, -d), zf)
     head_mf.wait_recv()
-    head_mff = same(wcap, 1 - yh, ring(z, -d), zf)
-    cores.append(same(wcap, 1 - yh, ring(z, -d), core))
+    head_mff = same(1 - yh, ring(z, -d), zf)
+    cores.append(same(1 - yh, ring(z, -d), core))
     xf2.wait_recv()
     xff2 = go(slot_rows(1, 96, CAP), slot_rows(0, 96, CAP), xf)
+    for copy in ihead[1:]:
+        copy.wait_recv()
+    icores = [many(x, core)]
+    icores += [many(ring(x, step), core, False) for step in (-d, d, 2)]
+    iway = [many(x, target) for target in (xf, xb, x2)]
     pyf1.wait_recv()
     pyff1 = p_y(ring(y, -d), yf, CUT // 2, CUT // 2)
     swaps.append(p_y(ring(y, -d), core))
@@ -240,14 +257,13 @@
     starts[1, 44:48, :] = jnp.full((4, 128), 1.0, F32)
 
     head_ff.wait_recv()
-    cores.append(same(wcap, yh, ring(z, 2), core))
+    cores.append(same(yh, ring(z, 2), core))
     head_mb.wait_recv()
-    cores.append(same(wcap, 1 - yh, ring(z, d), core))
+    cores.append(same(1 - yh, ring(z, d), core))
     pyb.wait_recv()
     swaps.append(p_y(ring(y, d), core))
     head_mff.wait_recv()
-    cores.append(same(wcap, 1 - yh, ring(z, 2), core))
-    ihead = head_start(wp, wimg, True)
+    cores.append(same(1 - yh, ring(z, 2), core))
     for copy in cores:
         copy.wait_recv()
 
@@ -273,13 +289,6 @@
     xff1.wait_recv()
     xff2.wait_recv()
     embed(slice(0, 2 * CAP))
-    ihead["m"].wait_recv()
-    ihead_m = [same(wimg, 1 - yh, z, target) for target in (zf, zb, z2)]
-    icores = [same(wimg, 1 - yh, z, core)]
-    for name, step in (("f", -d), ("b", d), ("2", 2)):
-        ihead[name].wait_recv()
-        icores.append(same(wimg, yh, ring(z, step), core))
-    icores_late = [same(wimg, 1 - yh, ring(z, step), core, False) for step in (-d, d, 2)]
     for copy in swaps:
         copy.wait_recv()
 
@@ -345,7 +354,7 @@
         def _():
             own_cap[...] = total[CAP : 2 * CAP]
             t3.start()
-            for arrived, copy in zip(ihead_m, icores_late):
+            for arrived, copy in zip(iway[0:2], icores[1:3]):
                 arrived.wait_recv()
                 copy.start()
 
@@ -363,7 +372,9 @@
         given.append(go(img_send.at[i], img_recv.at[i], core))
         if i == 0:
             img_own[0] = grad_rows(yl_, c)[0:IMG]
-    for copy in icores + icores_late:
+    iway[2].wait_recv()
+    icores[3].start()
+    for copy in icores:
         copy.wait_recv()
 
     def gp_part(y_):
@@ -481,6 +492,7 @@
     hbm = pl.BlockSpec(memory_space=pl.ANY)
     scratch = [
         ((IMG, D), BF),
+        ((D, SL), BF),
         ((4 * CAP, D), BF),
         ((D, D), BF),
         ((D, D), BF),

time: 66.3 us -> 64.2 us (0.968); the launches traced: 66.1 us -> 63.1 us
  Pallas kernels: 64.1 us -> 61.2 us
    pallas_call x1, Pallas kernels: 62.3 us -> 59.4 us  [body(): pl.pallas_call(kernel, out_shape=outs, in_specs=[hbm] * 4 + [vm] + [sm] *...]
where the time goes in v4:
time: 64.2 us; the launch traced here: 63.1 us
  Pallas kernels  61.2 us (95%)
  between operations  1.93 us (3%)
    pallas_call x1, Pallas kernels, body(): pl.pallas_call(kernel, out_shape=outs, in_specs=[hbm] * 4 + [vm] + [sm] *...  59.4 us
    pallas_call x1, Pallas kernels, body(): pl.pallas_call(finish, out_shape=outs, in_specs=[vm, vm], out_specs=(vm,...  1.81 us

profile of v4, /device:TPU:0, one launch (start us, length us, event | category | flops | bytes accessed | tf_op | source)
XLA Modules:
  0.0 63.1 jit_solution(15277444886978093419)
XLA Ops:
  1.9 59.4 %shard_map.86 = (bf16[352,128]{1,0:T(8,128)(2,1)}, bf16[176,1024]{1,0:T(8,128)(2,1)}) custom-call(bf16[352,1024]{1,0:T(8,128)(2,1)} %pic.1, bf16[176,1024]{1,0:T(8,128)(2,1)} %sent.1, bf16[1024,128]{1,0:T(8,128)(2,1)} %wp.1, bf16[1024,128]{1,0:T(8,128)(2,1)} %ws.1, s32[44,128]{1,0:T(8,128)} %bitcast.1, f32[1]{0:T(128)S(6)} %copy.9.sharp, f32[1]{0:T(128)S(6)} %copy.10.bias), custom_call_target="tpu_custom_call" | custom-call | tf_op jit(solution)/shard_map/pallas_call | solution.py:531
  61.3 1.8 %shard_map.87 = (bf16[352,128]{1,0:T(8,128)(2,1)}, bf16[176,1024]{1,0:T(8,128)(2,1)}) custom-call(bf16[352,128]{1,0:T(8,128)(2,1)} %get-tuple-element.4.img, bf16[176,1024]{1,0:T(8,128)(2,1)} %get-tuple-element.5.cap), custom_call_target="tpu_custom_call" | custom-call | tf_op jit(solution)/shard_map/pallas_call | solution.py:546

commit v5 on v4

--- a/solution.py
+++ b/solution.py
@@ -62,7 +62,6 @@
     own_p2,
     rpz,
     rqz,
-    tqz,
     gq2,
     own_q2,
     rqy,
@@ -404,24 +403,23 @@
 
     image_back(0, yl)
     py1 = go(gp_part(ring(y, 2)), rpy.at[0], yf)
-    qz1 = [go(gq.at[ring(z, 2), 0], rqz.at[0, 0], zf)]
-    qz3 = [go(gq.at[ring(z, -d), 0], rqz.at[2, 0], zb)]
+    qz = []
+
+    def q_first(i):
+        for n_, (step, target) in enumerate(((2, z2), (d, zf), (-d, zb))):
+            qz.append(go(gq.at[ring(z, step), i], rqz.at[n_, i], target))
+
+    q_first(0)
     img_own[1] = grad_rows(1 - yl, c)[0:IMG]
+    image_back(1, 1 - yl)
+    py3 = go(gp_part(ring(y, -d)), rpy.at[2], yb)
+    q_first(1)
     t1.wait_recv()
     cap_mid[...] = (part[2].astype(F32) + cap_in[0].astype(F32)).astype(BF)
     t2 = go(cap_mid, cap_in.at[1], xf)
-    image_back(1, 1 - yl)
-    py3 = go(gp_part(ring(y, -d)), rpy.at[2], yb)
-    qz1.append(go(gq.at[ring(z, 2), 1], rqz.at[0, 1], zf))
-    qz3.append(go(gq.at[ring(z, -d), 1], rqz.at[2, 1], zb))
     py1.wait_recv()
     tpy[...] = add(gp_part(ring(y, d))[...], rpy[0]).astype(BF)
     py2 = go(tpy, rpy.at[1], yf)
-    qz2 = []
-    for i in range(2):
-        qz1[i].wait_recv()
-        tqz[i] = add(gq[ring(z, d), i], rqz[0, i]).astype(BF)
-        qz2.append(go(tqz.at[i], rqz.at[1, i], zf))
 
     t2.wait_recv()
     t3.wait_recv()
@@ -449,9 +447,9 @@
         go(gp2.at[ring(z, -d)], rpz.at[2], zb),
     ]
     for i in range(2):
-        qz3[i].wait_recv()
-        qz2[i].wait_recv()
-        own = add(gq[z, i], rqz[1, i], rqz[2, i])
+        for copy in qz[3 * i : 3 * i + 3]:
+            copy.wait_recv()
+        own = add(gq[z, i], rqz[0, i], rqz[1, i], rqz[2, i])
         for yh_ in range(2):
             cut = own[yh_ * HALF : (yh_ + 1) * HALF]
             own_q2[i, yh_] = cut
@@ -517,7 +515,6 @@
         ((4, HALF, SL), F32),
         ((3, HALF, SL), BF),
         ((3, 2, 2 * HALF, SL), BF),
-        ((2, 2 * HALF, SL), BF),
         ((2, 2, HALF, SL), BF),
         ((2, 2, HALF, SL), F32),
         ((3, HALF, SL), BF),

time: 64.2 us -> 63.9 us (level)
  no operation moved by 1% of the time
where the time goes in v5:
time: 63.9 us; the launch traced here: 63.5 us
  Pallas kernels  61.5 us (96%)
  between operations  1.93 us (3%)
    pallas_call x1, Pallas kernels, body(): pl.pallas_call(kernel, out_shape=outs, in_specs=[hbm] * 4 + [vm] + [sm] *...  59.7 us
    pallas_call x1, Pallas kernels, body(): pl.pallas_call(finish, out_shape=outs, in_specs=[vm, vm], out_specs=(vm,...  1.81 us

profile of v5, /device:TPU:0, one launch (start us, length us, event | category | flops | bytes accessed | tf_op | source)
XLA Modules:
  0.0 63.5 jit_solution(13397892875217260357)
XLA Ops:
  1.9 59.7 %shard_map.86 = (bf16[352,128]{1,0:T(8,128)(2,1)}, bf16[176,1024]{1,0:T(8,128)(2,1)}) custom-call(bf16[352,1024]{1,0:T(8,128)(2,1)} %pic.1, bf16[176,1024]{1,0:T(8,128)(2,1)} %sent.1, bf16[1024,128]{1,0:T(8,128)(2,1)} %wp.1, bf16[1024,128]{1,0:T(8,128)(2,1)} %ws.1, s32[44,128]{1,0:T(8,128)} %bitcast.1, f32[1]{0:T(128)S(6)} %copy.9.sharp, f32[1]{0:T(128)S(6)} %copy.10.bias), custom_call_target="tpu_custom_call" | custom-call | tf_op jit(solution)/shard_map/pallas_call | solution.py:528
  61.7 1.8 %shard_map.87 = (bf16[352,128]{1,0:T(8,128)(2,1)}, bf16[176,1024]{1,0:T(8,128)(2,1)}) custom-call(bf16[352,128]{1,0:T(8,128)(2,1)} %get-tuple-element.4.img, bf16[176,1024]{1,0:T(8,128)(2,1)} %get-tuple-element.5.cap), custom_call_target="tpu_custom_call" | custom-call | tf_op jit(solution)/shard_map/pallas_call | solution.py:543

commit v6 on v5

--- a/solution.py
+++ b/solution.py
@@ -255,6 +255,36 @@
     starts[0, 44:48, :] = jnp.full((4, 128), -1.0, F32)
     starts[1, 44:48, :] = jnp.full((4, 128), 1.0, F32)
 
+    t = sharp[0]
+    shift = bias[0] * LOG2E
+    ones = jnp.ones((8, D), BF)
+    even = x % 2 == 0
+
+    def block_vec(which, yl_, c_):
+        row = (yl_ * 4 + x) * 2 + c_
+        q = (row * 11) // 4
+        v = jnp.concatenate([starts[which, pl.ds(q + i, 1), :] for i in range(4)], axis=1)
+        cuts = [((2 * p + 3 * c_) % 4) * 32 for p in range(2)]
+        return jnp.where(even, v[:, cuts[0] : cuts[0] + PAD], v[:, cuts[1] : cuts[1] + PAD])
+
+    for yl_ in range(2):
+        for c_ in range(2):
+            first = block_vec(0, yl_, c_)
+            num = block_vec(1, yl_, c_)
+            lanes = slice(c_ * PAD, (c_ + 1) * PAD)
+            vecs[yl_, 3:4, lanes] = first
+            vecs[yl_, 4:5, lanes] = first + num
+            vecs[yl_, 5:6, lanes] = -1.0 / num
+
+    def scales(yl_, c_):
+        zk = plane[pl.ds(mo((yl_ * 2 + c_) * PAD, PAD), PAD), :]
+        square = lax.dot_general(ones, zk * zk, NT, preferred_element_type=F32)
+        scale = t * lax.rsqrt(square[0:1, :] + EPS)
+        lanes = pl.ds(mo(c_ * PAD, PAD), PAD)
+        vecs[yl_, 0:1, lanes] = scale * LOG2E
+        vecs[yl_, 1:2, lanes] = scale
+        vecs[yl_, 2:3, lanes] = scale * vecs[yl_, 5:6, lanes]
+
     head_ff.wait_recv()
     cores.append(same(yh, ring(z, 2), core))
     head_mb.wait_recv()
@@ -285,38 +315,15 @@
     for yl_ in range(2):
         ref = plane.at[q_rows(yl_)]
         swaps.append(go(ref, ref, core))
+    for yl_ in range(2):
+        scales(yl_, c)
     xff1.wait_recv()
     xff2.wait_recv()
     embed(slice(0, 2 * CAP))
     for copy in swaps:
         copy.wait_recv()
-
-    t = sharp[0]
-    shift = bias[0] * LOG2E
-    ones = jnp.ones((8, D), BF)
-    even = x % 2 == 0
-
-    def block_vec(which, yl_, c_):
-        row = (yl_ * 4 + x) * 2 + c_
-        q = (row * 11) // 4
-        v = jnp.concatenate([starts[which, pl.ds(q + i, 1), :] for i in range(4)], axis=1)
-        cuts = [((2 * p + 3 * c_) % 4) * 32 for p in range(2)]
-        return jnp.where(even, v[:, cuts[0] : cuts[0] + PAD], v[:, cuts[1] : cuts[1] + PAD])
-
     for yl_ in range(2):
-        for c_ in range(2):
-            k = yl_ * 2 + c_
-            zk = plane[k * PAD : (k + 1) * PAD, :]
-            square = lax.dot_general(ones, zk * zk, NT, preferred_element_type=F32)
-            scale = t * lax.rsqrt(square[0:1, :] + EPS)
-            first = block_vec(0, yl_, c_)
-            num = block_vec(1, yl_, c_)
-            lanes = slice(c_ * PAD, (c_ + 1) * PAD)
-            vecs[yl_, 0:1, lanes] = scale * LOG2E
-            vecs[yl_, 1:2, lanes] = scale
-            vecs[yl_, 2:3, lanes] = -scale / num
-            vecs[yl_, 3:4, lanes] = first
-            vecs[yl_, 4:5, lanes] = first + num
+        scales(yl_, 1 - c)
 
     t1 = make(part.at[0], cap_in.at[0], xf)
     t3 = make(part.at[1], cap_in.at[2], xb)

time: 63.9 us -> 63.6 us (level)
  no operation moved by 1% of the time
where the time goes in v6:
time: 63.6 us; the launch traced here: 63.4 us
  Pallas kernels  61.5 us (97%)
  between operations  1.93 us (3%)
    pallas_call x1, Pallas kernels, body(): pl.pallas_call(kernel, out_shape=outs, in_specs=[hbm] * 4 + [vm] + [sm] *...  59.7 us
    pallas_call x1, Pallas kernels, body(): pl.pallas_call(finish, out_shape=outs, in_specs=[vm, vm], out_specs=(vm,...  1.81 us

profile of v6, /device:TPU:0, one launch (start us, length us, event | category | flops | bytes accessed | tf_op | source)
XLA Modules:
  0.0 63.4 jit_solution(13160810436294858759)
XLA Ops:
  1.9 59.7 %shard_map.86 = (bf16[352,128]{1,0:T(8,128)(2,1)}, bf16[176,1024]{1,0:T(8,128)(2,1)}) custom-call(bf16[352,1024]{1,0:T(8,128)(2,1)} %pic.1, bf16[176,1024]{1,0:T(8,128)(2,1)} %sent.1, bf16[1024,128]{1,0:T(8,128)(2,1)} %wp.1, bf16[1024,128]{1,0:T(8,128)(2,1)} %ws.1, s32[44,128]{1,0:T(8,128)} %bitcast.1, f32[1]{0:T(128)S(6)} %copy.9.sharp, f32[1]{0:T(128)S(6)} %copy.10.bias), custom_call_target="tpu_custom_call" | custom-call | tf_op jit(solution)/shard_map/pallas_call | solution.py:535
  61.6 1.8 %shard_map.87 = (bf16[352,128]{1,0:T(8,128)(2,1)}, bf16[176,1024]{1,0:T(8,128)(2,1)}) custom-call(bf16[352,128]{1,0:T(8,128)(2,1)} %get-tuple-element.4.img, bf16[176,1024]{1,0:T(8,128)(2,1)} %get-tuple-element.5.cap), custom_call_target="tpu_custom_call" | custom-call | tf_op jit(solution)/shard_map/pallas_call | solution.py:550
